TPU v7x, 256 devices: a whole 4x4x8 slice. The times are simulated.
256 devices in a mesh: rows: 64 (over z, y, core), tp: 4 (over x).
Axes of the slice: x: 4, y: 4, z: 8, core: 2. Of those that a mesh axis runs over, the one named last changes fastest.
Arguments:
- state_in: float32 [128, 64, 128, 256], P('rows', 'tp'), may hold values from -8 to 8
- tail_x: bfloat16 [128, 3, 64, 128], P('rows', None, 'tp'), may hold values from -6 to 6
- tail_bc: bfloat16 [128, 3, 2, 4, 256], P('rows'), may hold values from -6 to 6
- source: int32 [128], replicated, may hold values from 0 to 127, as said below
- active: int32 [128], P('rows'), may hold values 0 or 1
- x_new: bfloat16 [2, 128, 64, 128], P(None, 'rows', 'tp'), may hold values from -6 to 6
- z_new: bfloat16 [2, 128, 64, 128], P(None, 'rows', 'tp'), may hold values from -6 to 6
- bc_new: bfloat16 [2, 128, 2, 4, 256], P(None, 'rows'), may hold values from -6 to 6
- dt_new: float32 [2, 128, 128], P(None, 'rows'), may hold values from -6 to 6
- conv_wx: float32 [4, 64, 128], P(None, 'tp'), may hold values from -3 to 3
- conv_bx: float32 [64, 128], P('tp'), may hold values from -2 to 2
- conv_wbc: float32 [4, 2, 4, 256], replicated, may hold values from -3 to 3
- conv_bbc: float32 [2, 4, 256], replicated, may hold values from -2 to 2
- dt_bias: float32 [128], replicated, may hold values from -4 to -1
- a_log: float32 [128], replicated, may hold values from 0 to 2.5
- skip_d: float32 [128], replicated, may hold values from 0.5 to 2
- norm_gain: float32 [64, 128], P('tp'), may hold values from 0.1 to 1.9
Outputs:
- state_out: float32 [128, 64, 128, 256], P('rows', 'tp')
- tail_x_out: bfloat16 [128, 3, 64, 128], P('rows', None, 'tp')
- tail_bc_out: bfloat16 [128, 3, 2, 4, 256], P('rows')
- y_out: bfloat16 [2, 128, 64, 128], P(None, 'rows', 'tp')
Inputs may be any that keep to these rules, and one draw needn't show every extreme that they name: source is a permutation of the 128 slots; on each index of rows at most 1 of its 2 slots take a row held on another index, and as many give one away.
All inputs are finite; a program needn't handle non-finite values. No bound on the sum of `active` on one device may be relied on, other than what follows from the above.
Results may differ from a plain program's by a relative error of at most 0.0012.
Values sent between devices are 32-bit elements; how exact they have to be, the bound alone decides.
A program may use at most 128 MiB of HBM per device.

v0:
```python
import jax
import jax.numpy as jnp
from jax import lax
from jax.sharding import PartitionSpec as P

STEPS = 2


EPSILON = 1e-05


def packed_rows(state, tail_x, tail_bc, devices):
    count, depth_dev, head_count, state_width = state.shape
    piece_width = head_count // devices
    state_part = state.reshape(count, depth_dev, devices, piece_width, state_width)
    state_part = jnp.transpose(state_part, (0, 2, 1, 3, 4)).reshape(count, devices, -1)
    tail_part = tail_x.reshape(count, 3, depth_dev, devices, piece_width)
    tail_part = (
        jnp.transpose(tail_part, (0, 3, 1, 2, 4)).reshape(count, devices, -1).astype(jnp.float32)
    )
    bc_part = tail_bc.reshape(count, devices, -1).astype(jnp.float32)
    return jnp.concatenate([state_part, tail_part, bc_part], axis=2)


def unpacked_rows(buffer, count, devices, state_shape, tail_shape, bc_shape):
    depth_dev, head_count, state_width = state_shape
    piece_width = head_count // devices
    state_size = depth_dev * piece_width * state_width
    tail_size = 3 * depth_dev * piece_width
    state_part = buffer[:, :, :state_size].reshape(
        count, devices, depth_dev, piece_width, state_width
    )
    state_part = jnp.transpose(state_part, (0, 2, 1, 3, 4)).reshape((count,) + tuple(state_shape))
    tail_part = buffer[:, :, state_size : state_size + tail_size].reshape(
        count, devices, 3, depth_dev, piece_width
    )
    tail_part = (
        jnp.transpose(tail_part, (0, 2, 3, 1, 4))
        .reshape((count,) + tuple(tail_shape))
        .astype(jnp.bfloat16)
    )
    bc_part = (
        buffer[:, :, state_size + tail_size :]
        .reshape((count,) + tuple(bc_shape))
        .astype(jnp.bfloat16)
    )
    return (state_part, tail_part, bc_part)


def relocate(state_in, tail_x, tail_bc, source):
    devices = lax.axis_size("rows")
    slot_count = state_in.shape[0]
    state_shape = state_in.shape[1:]
    tail_shape = tail_x.shape[1:]
    bc_shape = tail_bc.shape[1:]
    outgoing = packed_rows(state_in, tail_x, tail_bc, devices)
    spread = lax.all_to_all(outgoing, "rows", split_axis=1, concat_axis=0, tiled=True)
    back = jnp.take(spread, source, axis=0).reshape((devices, slot_count) + spread.shape[1:])
    returned = lax.all_to_all(back, "rows", split_axis=0, concat_axis=2, tiled=True)
    buffer = returned.reshape(slot_count, devices, returned.shape[-1])
    return unpacked_rows(buffer, slot_count, devices, state_shape, tail_shape, bc_shape)


def on_device(
    state_in,
    tail_x,
    tail_bc,
    source,
    active,
    x_new,
    z_new,
    bc_new,
    dt_new,
    conv_wx,
    conv_bx,
    conv_wbc,
    conv_bbc,
    dt_bias,
    a_log,
    skip_d,
    norm_gain,
):
    state, window_x, window_bc = relocate(state_in, tail_x, tail_bc, source)
    slot_count, depth_dev, head_count, state_width = state.shape
    groups = conv_wbc.shape[2]
    per_group = head_count // groups
    full_depth = depth_dev * lax.axis_size("tp")
    live = active == 1
    live_state = live[:, None, None, None]
    live_bc = live[:, None, None, None, None]
    rate = jnp.exp(a_log)
    outputs = []
    for step_index in range(STEPS):
        entry_x = x_new[step_index]
        entry_bc = bc_new[step_index]
        frame_x = jnp.concatenate([window_x, entry_x[:, None]], axis=1).astype(jnp.float32)
        conv_x = jax.nn.silu(jnp.sum(frame_x * conv_wx[None], axis=1) + conv_bx)
        frame_bc = jnp.concatenate([window_bc, entry_bc[:, None]], axis=1).astype(jnp.float32)
        conv_bc = jax.nn.silu(jnp.sum(frame_bc * conv_wbc[None], axis=1) + conv_bbc)
        expand_b = jnp.repeat(conv_bc[:, 0], per_group, axis=1)
        expand_c = jnp.repeat(conv_bc[:, 1], per_group, axis=1)
        step_size = jax.nn.softplus(dt_new[step_index] + dt_bias)
        decay = jnp.exp(-step_size * rate)
        candidate = (
            state * decay[:, None, :, None]
            + (step_size[:, None, :] * conv_x)[..., None] * expand_b[:, None]
        )
        readout = jnp.sum(candidate * expand_c[:, None], axis=-1) + skip_d * conv_x
        gated = readout * jax.nn.silu(z_new[step_index].astype(jnp.float32))
        totals = lax.psum(
            jnp.sum(
                jnp.square(gated).reshape(slot_count, depth_dev, groups, per_group), axis=(1, 3)
            ),
            "tp",
        )
        factor = lax.rsqrt(totals / (full_depth * per_group) + EPSILON)
        scaled = gated * jnp.repeat(factor, per_group, axis=1)[:, None, :] * norm_gain
        outputs.append(jnp.where(live[:, None, None], scaled, 0.0).astype(jnp.bfloat16))
        state = jnp.where(live_state, candidate, state)
        window_x = jnp.where(
            live_state, jnp.concatenate([window_x[:, 1:], entry_x[:, None]], axis=1), window_x
        )
        window_bc = jnp.where(
            live_bc, jnp.concatenate([window_bc[:, 1:], entry_bc[:, None]], axis=1), window_bc
        )
    return (state, window_x, window_bc, jnp.stack(outputs))


def solution(mesh):
    return jax.shard_map(
        on_device,
        mesh=mesh,
        in_specs=(
            P("rows", "tp", None, None),
            P("rows", None, "tp", None),
            P("rows", None, None, None, None),
            P(),
            P("rows"),
            P(None, "rows", "tp", None),
            P(None, "rows", "tp", None),
            P(None, "rows", None, None, None),
            P(None, "rows", None),
            P(None, "tp", None),
            P("tp", None),
            P(),
            P(),
            P(),
            P(),
            P(),
            P("tp", None),
        ),
        out_specs=(
            P("rows", "tp", None, None),
            P("rows", None, "tp", None),
            P("rows", None, None, None, None),
            P(None, "rows", "tp", None),
        ),
        check_vma=False,
    )
```

profile of v0, /device:TPU:24, one launch (start us, length us, event | category | flops | bytes accessed | tf_op | source)
XLA Modules:
  0.0 363.5 jit_solution(13979576972804627725)
XLA Ops:
  0.6 5.8 %reshape.412 = f32[2,16,64,2,256]{4,3,2,1,0:T(2,128)} reshape(f32[2,16,128,256]{3,2,1,0:T(8,128)} %param.17) | data formatting | bytes 8388608 | tf_op jit(solution)/shard_map/reshape | solution.py:15
  6.4 6.5 %copy.219 = f32[2,64,16,2,256]{4,3,2,0,1:T(2,128)} copy(f32[2,64,16,2,256]{4,3,1,2,0:T(2,128)} %bitcast.98) | data formatting | bytes 8388608 | tf_op jit(solution)/shard_map/transpose | solution.py:16
  13.0 7.5 %reshape.413 = f32[2,64,8192]{2,0,1:T(2,128)} reshape(f32[2,64,16,2,256]{4,3,2,0,1:T(2,128)} %copy.219) | data formatting | bytes 8388608 | tf_op jit(solution)/shard_map/reshape | solution.py:16
  21.1 14.6 %concatenate.27 = f32[2,64,8384]{2,0,1:T(2,128)} concatenate(f32[2,64,8192]{2,0,1:T(2,128)} %reshape.413, f32[2,64,96]{2,0,1:T(2,128)S(1)} %copy.222, f32[2,64,96]{2,0,1:T(2,128)S(1)} %copy.223), dimensions={2} | concatenate | bytes 8585216 | tf_op jit(solution)/shard_map/concatenate | solution.py:22
  35.7 12.2 %all-to-all-start = ((f32[2,64,8384]{2,0,1:T(2,128)}), f32[2,64,8384]{2,0,1:T(2,128)}, u32[]{:S(2)}, u32[]{:S(2)}) async-start(f32[2,64,8384]{2,0,1:T(2,128)} %concatenate.27), calls=%async_computation | async-start | bytes 8650752 | tf_op jit(solution)/shard_map/all_to_all | solution.py:57
  48.1 98.8 %all-to-all-done = f32[2,64,8384]{2,0,1:T(2,128)} async-done(((f32[2,64,8384]{2,0,1:T(2,128)}), f32[2,64,8384]{2,0,1:T(2,128)}, u32[]{:S(2)}, u32[]{:S(2)}) %all-to-all-start) | async-done | bytes 4292640 | tf_op jit(solution)/shard_map/all_to_all | solution.py:57
  146.8 6.2 %reshape.422 = f32[128,8384]{1,0:T(8,128)} reshape(f32[64,2,1,8384]{3,1,0,2:T(2,128)} %bitcast.5) | data formatting | bytes 8585216 | tf_op jit(solution)/shard_map/all_to_all | solution.py:57
  153.1 7.9 %gather_fusion = f32[128,8384]{1,0:T(8,128)} fusion(f32[128,8384]{1,0:T(8,128)} %reshape.422, s32[1024]{0:T(1024)S(1)} %pad_clamp_fusion), kind=kCustom, calls=%fused_computation | custom fusion | bytes 8585728 | tf_op jit(solution)/shard_map/jit(_take)/gather | solution.py:58
  161.0 5.9 %gather.7 = f32[64,2,1,8384]{3,1,0,2:T(2,128)} reshape(f32[128,8384]{1,0:T(8,128)} %gather_fusion) | data formatting | bytes 8585216 | tf_op jit(solution)/shard_map/jit(_take)/gather | solution.py:58
  166.9 6.5 %select_bitcast_fusion = f32[64,2,1,8384]{3,1,2,0:T(2,128)} fusion(f32[64,2,1,8384]{3,1,0,2:T(2,128)} %gather.7, pred[64,2]{1,0:T(8,128)(4,1)S(1)} %broadcast_in_dim.122), kind=kLoop, calls=%fused_computation.1 | loop fusion | flops 1073152 | bytes 8585344 | tf_op jit(solution)/shard_map/jit(_take)/select_n | solution.py:58
  173.5 5.8 %all-to-all-start.1 = ((f32[64,2,1,8384]{3,1,2,0:T(2,128)}), f32[64,2,1,8384]{3,1,2,0:T(2,128)}, u32[]{:S(2)}, u32[]{:S(2)}) async-start(f32[64,2,1,8384]{3,1,2,0:T(2,128)} %select_bitcast_fusion), calls=%async_computation.1 | async-start | bytes 8650752 | tf_op jit(solution)/shard_map/all_to_all | solution.py:59
  180.9 0.7 copy.239
  181.7 0.7 copy.257
  182.5 0.7 copy.253
  183.3 0.7 copy.268
  184.1 0.6 copy.249
  185.4 92.9 %all-to-all-done.1 = f32[64,2,1,8384]{3,1,2,0:T(2,128)} async-done(((f32[64,2,1,8384]{3,1,2,0:T(2,128)}), f32[64,2,1,8384]{3,1,2,0:T(2,128)}, u32[]{:S(2)}, u32[]{:S(2)}) %all-to-all-start.1) | async-done | bytes 4292640 | tf_op jit(solution)/shard_map/all_to_all | solution.py:59
  278.4 8.9 %copy.225 = f32[64,2,1,8384]{0,3,1,2:T(8,128)} copy(f32[64,2,1,8384]{3,1,2,0:T(2,128)} %all-to-all-done.1) | data formatting | bytes 8585216 | tf_op jit(solution)/shard_map/all_to_all | solution.py:59
  287.3 3.9 %bitcast_convert_fusion = bf16[2,64,8384]{1,2,0:T(8,128)(2,1)S(1)} fusion(f32[64,2,1,8384]{0,3,1,2:T(8,128)} %copy.225), kind=kLoop, calls=%fused_computation.60 | loop fusion | flops 1073152 | bytes 6438912 | tf_op jit(solution)/shard_map/convert.7
  293.2 1.0 copy.244
  294.2 1.8 copy.260
  296.0 7.2 %slice.80 = f32[2,64,8192]{1,2,0:T(8,128)} slice(f32[2,64,8384]{1,2,0:T(8,128)} %bitcast.94), slice={[0:2], [0:64], [0:8192]} | slice | bytes 8388608 | tf_op jit(solution)/shard_map/slice | solution.py:30
  303.2 8.6 %copy.226 = f32[2,64,16,2,256]{4,3,2,0,1:T(2,128)} copy(f32[2,64,16,2,256]{1,4,3,2,0:T(8,128)} %bitcast.95) | data formatting | bytes 8388608 | tf_op jit(solution)/shard_map/reshape | solution.py:30
  312.0 15.6 %multiply_reduce_fusion = (f32[2,16,64,2]{3,1,0,2:T(8,128)S(1)}, f32[2,16,64,2]{3,1,0,2:T(8,128)S(1)}) fusion(f32[2,64,16,2,256]{4,3,2,0,1:T(2,128)} %copy.226, f32[2,64,256]{2,0,1:T(2,128)S(1)} %bitcast.111, f32[2,64,256]{2,0,1:T(2,128)S(1)} %bitcast.109, f32[2,16,64,2]{3,1,0,2:T(8,128)S(1)} %copy.244, f32[2,64,2]{2,0,1:T(2,128)} %copy.239, ...), kind=kLoop, calls=%fused_computation.8 | loop fusion | flops 11526144 | bytes 4786178 | tf_op jit(solution)/shard_map/reduce_sum | solution.py:108
  328.2 0.8 copy.247
  329.7 0.8 copy.263
  330.5 8.5 %copy.272 = f32[2,64,16,2,256]{4,3,1,2,0:T(2,128)} copy(f32[2,64,16,2,256]{1,4,3,2,0:T(8,128)} %bitcast.96) | data formatting | bytes 8388608 | tf_op jit(solution)/shard_map/transpose | solution.py:33
  339.6 10.5 %all-reduce = (f32[2,4]{1,0:T(2,128)S(1)}, f32[2,4]{1,0:T(2,128)S(1)}) all-reduce(f32[2,4]{1,0:T(2,128)S(1)} %copy.278, f32[2,4]{1,0:T(2,128)S(1)} %copy.276), channel_id=1, replica_groups=mesh['rows'=64,'tp'=4] {'tp'}, use_global_device_ids=true, to_apply=%region_11.12 | all-reduce | flops 16 | bytes 128 | tf_op jit(solution)/shard_map/psum | solution.py:110
  350.7 6.2 %reshape.416 = f32[2,16,128,256]{3,2,1,0:T(8,128)} reshape(f32[2,16,64,2,256]{4,3,2,1,0:T(2,128)} %bitcast.97) | data formatting | bytes 8388608 | tf_op jit(solution)/shard_map/reshape | solution.py:33
  356.9 0.7 maximum_select_fusion.3
  357.7 0.7 copy.271
  359.2 4.3 %add_select_fusion = f32[2,16,128,256]{3,2,1,0:T(8,128)} fusion(f32[2,16,128,256]{3,2,1,0:T(8,128)} %reshape.416, f32[2,128,256]{2,1,0:T(8,128)S(1)} %bitcast.104, f32[2,16,128]{2,1,0:T(8,128)S(1)} %get-tuple-element.63, f32[2,128]{1,0:T(2,128)S(1)} %copy-done.27, f32[2,128,256]{2,1,0:T(8,128)S(1)} %bitcast.103, f32[2,16,128]{2,1,0:T(8,128)S(1)} %get-tuple-element.62, ...), kind=kLoop, calls=%fused_computation.9 | loop fusion | flops 8388608 | bytes 8947714 | tf_op jit(solution)/shard_map/jit(_where)/select_n | solution.py:119
  (162 shorter events, 8.5 us)
Async XLA Ops:
  13.0 7.5 %copy-start.19 = (bf16[2,3,16,128]{3,2,1,0:T(8,128)(2,1)S(1)}, bf16[2,3,16,128]{3,2,1,0:T(8,128)(2,1)}, u32[]{:S(2)}) copy-start(bf16[2,3,16,128]{3,2,1,0:T(8,128)(2,1)} %param.18) | copy-start | bytes 73732
  13.0 7.9 %copy-start.20 = (bf16[2,3,2,4,256]{4,3,2,1,0:T(4,128)(2,1)S(1)}, bf16[2,3,2,4,256]{4,3,2,1,0:T(4,128)(2,1)}, u32[]{:S(2)}) copy-start(bf16[2,3,2,4,256]{4,3,2,1,0:T(4,128)(2,1)} %param.19) | copy-start | bytes 73732
  35.7 12.2 %copy-start.34 = (s32[128]{0:T(128)S(1)}, s32[128]{0:T(128)}, u32[]{:S(2)}) copy-start(s32[128]{0:T(128)} %param.20) | copy-start | bytes 1540
  35.7 111.2 %all-to-all-start = ((f32[2,64,8384]{2,0,1:T(2,128)}), f32[2,64,8384]{2,0,1:T(2,128)}, u32[]{:S(2)}, u32[]{:S(2)}) async-start(f32[2,64,8384]{2,0,1:T(2,128)} %concatenate.27), calls=%async_computation | async-start | bytes 8650752 | tf_op jit(solution)/shard_map/all_to_all | solution.py:57
  173.4 6.4 %copy-start.25 = (f32[2,2,128]{2,1,0:T(2,128)S(1)}, f32[2,2,128]{2,1,0:T(2,128)}, u32[]{:S(2)}) copy-start(f32[2,2,128]{2,1,0:T(2,128)} %param.25) | copy-start | bytes 6148
  173.4 6.8 %copy-start.35 = (f32[128]{0:T(128)S(1)}, f32[128]{0:T(128)}, u32[]{:S(2)}) copy-start(f32[128]{0:T(128)} %param.31) | copy-start | bytes 1540
  173.4 7.1 %copy-start.33 = (f32[128]{0:T(128)S(1)}, f32[128]{0:T(128)}, u32[]{:S(2)}) copy-start(f32[128]{0:T(128)} %param.30) | copy-start | bytes 1540
  173.4 7.3 %copy-start.6 = (f32[16,128]{1,0:T(8,128)S(1)}, f32[16,128]{1,0:T(8,128)}, u32[]{:S(2)}) copy-start(f32[16,128]{1,0:T(8,128)} %param.27) | copy-start | bytes 24580
  173.4 9.0 %copy-start.13 = (bf16[2,2,16,128]{3,2,1,0:T(8,128)(2,1)S(1)}, bf16[2,2,16,128]{3,2,1,0:T(8,128)(2,1)}, u32[]{:S(2)}) copy-start(bf16[2,2,16,128]{3,2,1,0:T(8,128)(2,1)} %param.23) | copy-start | bytes 49156
  173.4 10.6 %copy-start.31 = (f32[128]{0:T(128)S(1)}, f32[128]{0:T(128)}, u32[]{:S(2)}) copy-start(f32[128]{0:T(128)} %param.32) | copy-start | bytes 1540
  173.4 11.3 %copy-start.36 = (s32[2]{0:T(128)S(1)}, s32[2]{0:T(128)}, u32[]{:S(2)}) copy-start(s32[2]{0:T(128)} %param.21) | copy-start | bytes 28
  173.5 12.0 %copy-start.22 = (bf16[2,2,2,4,256]{4,3,2,1,0:T(4,128)(2,1)S(1)}, bf16[2,2,2,4,256]{4,3,2,1,0:T(4,128)(2,1)}, u32[]{:S(2)}) copy-start(bf16[2,2,2,4,256]{4,3,2,1,0:T(4,128)(2,1)} %param.24) | copy-start | bytes 49156
  173.5 104.9 %all-to-all-start.1 = ((f32[64,2,1,8384]{3,1,2,0:T(2,128)}), f32[64,2,1,8384]{3,1,2,0:T(2,128)}, u32[]{:S(2)}, u32[]{:S(2)}) async-start(f32[64,2,1,8384]{3,1,2,0:T(2,128)} %select_bitcast_fusion), calls=%async_computation.1 | async-start | bytes 8650752 | tf_op jit(solution)/shard_map/all_to_all | solution.py:59
  184.8 107.2 %copy-start.17 = (pred[2]{0:T(512)(128)(4,1)}, pred[2]{0:T(512)(128)(4,1)S(1)}, u32[]{:S(2)}) copy-start(pred[2]{0:T(512)(128)(4,1)S(1)} %broadcast_compare_fusion) | copy-start | bytes 10
  185.4 106.4 %copy-start.7 = (bf16[2,1,2,4,256]{4,3,2,1,0:T(4,128)(2,1)}, bf16[2,1,2,4,256]{4,3,2,1,0:T(4,128)(2,1)S(1)}, u32[]{:S(2)}) copy-start(bf16[2,1,2,4,256]{4,3,2,1,0:T(4,128)(2,1)S(1)} %get-tuple-element.60) | copy-start | bytes 24580
  291.8 47.3 %copy-start.2 = (bf16[2,3,2,4,256]{4,3,2,1,0:T(4,128)(2,1)}, bf16[2,3,2,4,256]{4,3,2,1,0:T(4,128)(2,1)S(1)}, u32[]{:S(2)}) copy-start(bf16[2,3,2,4,256]{4,3,2,1,0:T(4,128)(2,1)S(1)} %maximum_select_fusion.2) | copy-start | bytes 73732
  292.6 47.0 %copy-start = (bf16[2,3,16,128]{2,3,1,0:T(8,128)(2,1)}, bf16[2,3,16,128]{2,3,1,0:T(8,128)(2,1)S(1)}, u32[]{:S(2)}) copy-start(bf16[2,3,16,128]{2,3,1,0:T(8,128)(2,1)S(1)} %maximum_select_fusion) | copy-start | bytes 73732
  330.5 8.6 %copy-start.4 = (f32[2,16,64,2]{2,1,3,0:T(8,128)S(1)}, f32[2,16,64,2]{2,1,3,0:T(8,128)}, u32[]{:S(2)}) copy-start(f32[2,16,64,2]{2,1,3,0:T(8,128)} %copy.253) | copy-start | bytes 49156
  330.5 8.6 %copy-start.5 = (f32[2,16,64,2]{2,1,3,0:T(8,128)S(1)}, f32[2,16,64,2]{2,1,3,0:T(8,128)}, u32[]{:S(2)}) copy-start(f32[2,16,64,2]{2,1,3,0:T(8,128)} %copy.268) | copy-start | bytes 49156
  330.5 8.6 %copy-start.30 = (f32[64,2]{0,1:T(2,128)S(1)}, f32[64,2]{0,1:T(2,128)}, u32[]{:S(2)}) copy-start(f32[64,2]{0,1:T(2,128)} %copy.249) | copy-start | bytes 1540
  350.5 6.3 %copy-start.8 = (bf16[2,1,2,4,256]{4,3,2,1,0:T(4,128)(2,1)S(1)}, bf16[2,1,2,4,256]{4,3,2,1,0:T(4,128)(2,1)}, u32[]{:S(2)}) copy-start(bf16[2,1,2,4,256]{4,3,2,1,0:T(4,128)(2,1)} %copy-done.7) | copy-start | bytes 24580
  350.5 7.0 %copy-start.1 = (bf16[2,3,16,128]{2,3,1,0:T(8,128)(2,1)S(1)}, bf16[2,3,16,128]{2,3,1,0:T(8,128)(2,1)}, u32[]{:S(2)}) copy-start(bf16[2,3,16,128]{2,3,1,0:T(8,128)(2,1)} %copy-done) | copy-start | bytes 73732
  350.6 7.0 %slice-start = ((bf16[2,3,16,128]{2,3,1,0:T(8,128)(2,1)}), bf16[2,2,16,128]{2,3,1,0:T(8,128)(2,1)S(1)}, s32[]{:S(2)}) async-start(bf16[2,3,16,128]{2,3,1,0:T(8,128)(2,1)} %copy-done), calls=%async_computation.2 | async-start | bytes 262144 | tf_op jit(solution)/shard_map/slice | solution.py:121
  350.6 7.8 %copy-start.14 = (bf16[2,2,16,128]{3,2,1,0:T(8,128)(2,1)S(1)}, bf16[2,2,16,128]{3,2,1,0:T(8,128)(2,1)}, u32[]{:S(2)}) copy-start(bf16[2,2,16,128]{3,2,1,0:T(8,128)(2,1)} %param.23) | copy-start | bytes 49156
  350.6 7.8 %copy-start.23 = (f32[16,128]{1,0:T(8,128)S(1)}, f32[16,128]{1,0:T(8,128)}, u32[]{:S(2)}) copy-start(f32[16,128]{1,0:T(8,128)} %param.33) | copy-start | bytes 24580
  350.6 7.8 %copy-start.32 = (f32[128]{0:T(128)S(1)}, f32[128]{0:T(128)}, u32[]{:S(2)}) copy-start(f32[128]{0:T(128)} %param.32) | copy-start | bytes 1540
  350.6 8.5 %copy-start.28 = (f32[2,128]{1,0:T(2,128)S(1)}, f32[2,128]{1,0:T(2,128)}, u32[]{:S(2)}) copy-start(f32[2,128]{1,0:T(2,128)} %get-tuple-element.43) | copy-start | bytes 3076
  350.6 8.5 %copy-start.29 = (f32[2,128]{1,0:T(2,128)S(1)}, f32[2,128]{1,0:T(2,128)}, u32[]{:S(2)}) copy-start(f32[2,128]{1,0:T(2,128)} %get-tuple-element.67) | copy-start | bytes 3076
  350.6 8.5 %copy-start.12 = (f32[2,4,256]{2,1,0:T(4,128)S(1)}, f32[2,4,256]{2,1,0:T(4,128)}, u32[]{:S(2)}) copy-start(f32[2,4,256]{2,1,0:T(4,128)} %copy-done.11) | copy-start | bytes 24580
  350.6 8.5 %copy-start.10 = (f32[2,4,256]{2,1,0:T(4,128)S(1)}, f32[2,4,256]{2,1,0:T(4,128)}, u32[]{:S(2)}) copy-start(f32[2,4,256]{2,1,0:T(4,128)} %copy-done.9) | copy-start | bytes 24580
  350.6 8.6 %copy-start.26 = (f32[2,128]{1,0:T(2,128)S(1)}, f32[2,128]{1,0:T(2,128)}, u32[]{:S(2)}) copy-start(f32[2,128]{1,0:T(2,128)} %get-tuple-element.42) | copy-start | bytes 3076
  350.7 8.6 %copy-start.27 = (f32[2,128]{1,0:T(2,128)S(1)}, f32[2,128]{1,0:T(2,128)}, u32[]{:S(2)}) copy-start(f32[2,128]{1,0:T(2,128)} %get-tuple-element.66) | copy-start | bytes 3076
  (9 other events, 41.1 us)
where the time goes:
time: 366 us; the launch traced here: 363 us
  waiting for transfers between devices  192 us (52%)
  local copies, waits for them, and re-layouts  109 us (30%)
  other arithmetic  32.9 us (9%)
  starting transfers between devices  18 us (5%)
  blocking collectives  10.5 us (3%)
    all_to_all x1, waiting for transfers between devices, relocate(): lax.all_to_all(outgoing, 'rows', split_axis=1, concat_axis=0, tiled=True)  98.8 us
    all_to_all x1, waiting for transfers between devices, relocate(): lax.all_to_all(back, 'rows', split_axis=0, concat_axis=2, tiled=True)  92.9 us
    reduce_sum x1, other arithmetic, on_device(): readout = jnp.sum(candidate * expand_c[:, None], axis=-1) + skip_d * conv_x  15.6 us
    concatenate x1, local copies, waits for them, and re-layouts, packed_rows(): return jnp.concatenate([state_part, tail_part, bc_part], axis=2)  14.6 us
    gather x2, local copies, waits for them, and re-layouts, relocate(): jnp.take(spread, source, axis=0)  13.8 us
    all_to_all x1, starting transfers between devices, relocate(): lax.all_to_all(outgoing, 'rows', split_axis=1, concat_axis=0, tiled=True)  12.2 us
    psum x1, blocking collectives, on_device(): lax.psum(jnp.sum(jnp.square(gated).reshape(slot_count, depth_dev, groups,...  10.5 us
    all_to_all x1, local copies, waits for them, and re-layouts, relocate(): lax.all_to_all(back, 'rows', split_axis=0, concat_axis=2, tiled=True)  8.9 us
  transfers between devices with their start and end apart: 2, of which 2 were waited for; matrix products, arithmetic and copies ran while one was open for 2% of the time, Pallas kernels for 0%

commit v1 on v0

--- a/solution.py
+++ b/solution.py
@@ -1,64 +1,214 @@
+import functools
 import jax
 import jax.numpy as jnp
 from jax import lax
+from jax.experimental import pallas as pl
+from jax.experimental.pallas import tpu as pltpu
 from jax.sharding import PartitionSpec as P
 
 STEPS = 2
-
-
 EPSILON = 1e-05
-
-
-def packed_rows(state, tail_x, tail_bc, devices):
-    count, depth_dev, head_count, state_width = state.shape
-    piece_width = head_count // devices
-    state_part = state.reshape(count, depth_dev, devices, piece_width, state_width)
-    state_part = jnp.transpose(state_part, (0, 2, 1, 3, 4)).reshape(count, devices, -1)
-    tail_part = tail_x.reshape(count, 3, depth_dev, devices, piece_width)
-    tail_part = (
-        jnp.transpose(tail_part, (0, 3, 1, 2, 4)).reshape(count, devices, -1).astype(jnp.float32)
+MESH = pl.DeviceIdType.MESH
+CHUNKS = 2
+TAIL_ROWS = 2
+
+
+def partner_of(me, i, devices):
+    return lax.rem(me + i, devices)
+
+
+def relocate_kernel(
+    devices,
+    heads,
+    source,
+    state_hbm,
+    tail_x,
+    tail_bc,
+    moved,
+    tails_out,
+    state,
+    tails,
+    first_a,
+    first_b,
+    spread_a,
+    spread_b,
+    second_a,
+    second_b,
+    back_a,
+    back_b,
+    load_sem,
+    send_sem,
+    recv_sem,
+):
+    me = lax.axis_index("rows")
+    part = heads // CHUNKS
+    lanes = 128
+    first, spread, second, back = (
+        (first_a, first_b),
+        (spread_a, spread_b),
+        (second_a, second_b),
+        (back_a, back_b),
     )
-    bc_part = tail_bc.reshape(count, devices, -1).astype(jnp.float32)
-    return jnp.concatenate([state_part, tail_part, bc_part], axis=2)
-
-
-def unpacked_rows(buffer, count, devices, state_shape, tail_shape, bc_shape):
-    depth_dev, head_count, state_width = state_shape
-    piece_width = head_count // devices
-    state_size = depth_dev * piece_width * state_width
-    tail_size = 3 * depth_dev * piece_width
-    state_part = buffer[:, :, :state_size].reshape(
-        count, devices, depth_dev, piece_width, state_width
-    )
-    state_part = jnp.transpose(state_part, (0, 2, 1, 3, 4)).reshape((count,) + tuple(state_shape))
-    tail_part = buffer[:, :, state_size : state_size + tail_size].reshape(
-        count, devices, 3, depth_dev, piece_width
-    )
-    tail_part = (
-        jnp.transpose(tail_part, (0, 2, 3, 1, 4))
-        .reshape((count,) + tuple(tail_shape))
-        .astype(jnp.bfloat16)
-    )
-    bc_part = (
-        buffer[:, :, state_size + tail_size :]
-        .reshape((count,) + tuple(bc_shape))
-        .astype(jnp.bfloat16)
-    )
-    return (state_part, tail_part, bc_part)
+    load = pltpu.make_async_copy(state_hbm, state, load_sem)
+    load.start()
+    barrier = pltpu.get_barrier_semaphore()
+
+    def greet(i, carry):
+        pl.semaphore_signal(
+            barrier,
+            inc=1,
+            device_id={"rows": partner_of(me, i, devices)},
+            device_id_type=MESH,
+        )
+        return carry
+
+    lax.fori_loop(1, devices, greet, 0)
+
+    low = source[2 * me]
+    high = source[2 * me + 1]
+    given = jnp.where((low != 2 * me) & (high != 2 * me), 0, 1)
+
+    for k in range(3):
+        tails[16 * k : 16 * k + 16, :] = tail_x[given, k].astype(jnp.float32)
+        for b in range(2):
+            entry = tail_bc[given, k, b].astype(jnp.float32)
+            at = 48 + (2 * k + b) * 8
+            tails[at : at + 4, :] = entry[:, :lanes]
+            tails[at + 4 : at + 8, :] = entry[:, lanes:]
+
+    def remote(phase, chunk, to):
+        source_ref, target_ref = ((first, spread), (second, back))[phase]
+        return pltpu.make_async_remote_copy(
+            src_ref=source_ref[chunk].at[to],
+            dst_ref=target_ref[chunk].at[me],
+            send_sem=send_sem.at[phase, chunk],
+            recv_sem=recv_sem.at[phase, chunk],
+            device_id={"rows": to},
+            device_id_type=MESH,
+        )
+
+    def all_pieces(phase, chunk):
+        source_ref, target_ref = ((first, spread), (second, back))[phase]
+        return pltpu.make_async_remote_copy(
+            src_ref=source_ref[chunk].at[pl.ds(0, devices - 1)],
+            dst_ref=target_ref[chunk].at[pl.ds(0, devices - 1)],
+            send_sem=send_sem.at[phase, chunk],
+            recv_sem=recv_sem.at[phase, chunk],
+            device_id={"rows": partner_of(me, 1, devices)},
+            device_id_type=MESH,
+        )
+
+    def pack(chunk, piece, into, at):
+        rows = state[given, piece, chunk * part : (chunk + 1) * part, :]
+        into[at, 0:part, :] = rows[:, :lanes]
+        into[at, part : 2 * part, :] = rows[:, lanes:]
+        if chunk == 0:
+            into[at, 2 * part, :] = tails[piece, :]
+            into[at, 2 * part + 1, :] = tails[64 + lax.rem(piece, 32), :]
+
+    load.wait()
+    pl.semaphore_wait(barrier, devices - 1)
+    for chunk in range(CHUNKS):
+
+        def begin(i, carry, chunk=chunk):
+            to = partner_of(me, i, devices)
+            pack(chunk, to, first[chunk], to)
+            remote(0, chunk, to).start()
+            return carry
+
+        lax.fori_loop(1, devices, begin, 0)
+        pack(chunk, me, spread[chunk], me)
+
+    def giver(to):
+        from_low = lax.shift_right_logical(source[2 * to], 1)
+        from_high = lax.shift_right_logical(source[2 * to + 1], 1)
+        return jnp.where(from_low != to, from_low, from_high)
+
+    for chunk in range(CHUNKS):
+        all_pieces(0, chunk).wait_recv()
+
+        def forward(i, carry, chunk=chunk):
+            to = partner_of(me, i, devices)
+            second[chunk][to] = spread[chunk][giver(to)]
+            remote(1, chunk, to).start()
+            return carry
+
+        lax.fori_loop(1, devices, forward, 0)
+        back[chunk][me] = spread[chunk][giver(me)]
+
+    for chunk in range(CHUNKS):
+        all_pieces(1, chunk).wait_recv()
+
+        def unpack(k, carry, chunk=chunk):
+            moved[k, chunk * part : (chunk + 1) * part, 0:lanes] = back[chunk][k, 0:part, :]
+            moved[k, chunk * part : (chunk + 1) * part, lanes:] = back[chunk][
+                k, part : 2 * part, :
+            ]
+            if chunk == 0:
+                tails_out[64 + lax.rem(k, 32), :] = back[0][k, 2 * part + 1, :]
+                tails_out[k, :] = back[0][k, 2 * part, :]
+            return carry
+
+        lax.fori_loop(0, devices, unpack, 0)
+
+    for phase in range(2):
+        for chunk in range(CHUNKS):
+            all_pieces(phase, chunk).wait_send()
 
 
 def relocate(state_in, tail_x, tail_bc, source):
     devices = lax.axis_size("rows")
-    slot_count = state_in.shape[0]
-    state_shape = state_in.shape[1:]
-    tail_shape = tail_x.shape[1:]
-    bc_shape = tail_bc.shape[1:]
-    outgoing = packed_rows(state_in, tail_x, tail_bc, devices)
-    spread = lax.all_to_all(outgoing, "rows", split_axis=1, concat_axis=0, tiled=True)
-    back = jnp.take(spread, source, axis=0).reshape((devices, slot_count) + spread.shape[1:])
-    returned = lax.all_to_all(back, "rows", split_axis=0, concat_axis=2, tiled=True)
-    buffer = returned.reshape(slot_count, devices, returned.shape[-1])
-    return unpacked_rows(buffer, slot_count, devices, state_shape, tail_shape, bc_shape)
+    slots, depth, head_count, width = state_in.shape
+    heads = depth * head_count // devices
+    part = heads // CHUNKS
+    pieces = state_in.reshape(slots, devices, heads, width)
+    long_buffer = pltpu.VMEM((devices, 2 * part + TAIL_ROWS, 128), jnp.float32)
+    short_buffer = pltpu.VMEM((devices, 2 * part, 128), jnp.float32)
+    vmem = pl.BlockSpec(memory_space=pltpu.VMEM)
+    moved, tails = pl.pallas_call(
+        functools.partial(relocate_kernel, devices, heads),
+        out_shape=(
+            jax.ShapeDtypeStruct((devices, heads, width), jnp.float32),
+            jax.ShapeDtypeStruct((96, 128), jnp.float32),
+        ),
+        in_specs=[
+            pl.BlockSpec(memory_space=pltpu.SMEM),
+            pl.BlockSpec(memory_space=pl.ANY),
+            vmem,
+            vmem,
+        ],
+        out_specs=(vmem, vmem),
+        scratch_shapes=[
+            pltpu.VMEM((slots, devices, heads, width), jnp.float32),
+            pltpu.VMEM((96, 128), jnp.float32),
+        ]
+        + [long_buffer, short_buffer] * 4
+        + [
+            pltpu.SemaphoreType.DMA,
+            pltpu.SemaphoreType.DMA((2, CHUNKS)),
+            pltpu.SemaphoreType.DMA((2, CHUNKS)),
+        ],
+        compiler_params=pltpu.CompilerParams(
+            collective_id=0, has_side_effects=True, vmem_limit_bytes=48 * 1024 * 1024
+        ),
+    )(source, pieces, tail_x, tail_bc)
+    me = lax.axis_index("rows")
+    mine = lax.dynamic_slice(source, (2 * me,), (2,))
+    local = mine - 2 * me
+    here = (local >= 0) & (local < slots)
+    safe = jnp.clip(local, 0, slots - 1)
+    moved = moved.reshape(depth, head_count, width)
+    moved_x = tails[:48].reshape(3, depth, head_count).astype(jnp.bfloat16)
+    halves = tails[48:].reshape(3, 2, 2, 4, 128)
+    moved_bc = jnp.transpose(halves, (0, 1, 3, 2, 4)).reshape(3, 2, 4, 256).astype(jnp.bfloat16)
+
+    def pick(array, new):
+        swapped = jnp.where(
+            (safe == 0).reshape((2,) + (1,) * new.ndim), array[0][None], array[1][None]
+        )
+        return jnp.where(here.reshape((2,) + (1,) * new.ndim), swapped, new[None])
+
+    return pick(state_in, moved), pick(tail_x, moved_x), pick(tail_bc, moved_bc)
 
 
 def on_device(

time: 366 us -> 135 us (0.37)
  waiting for transfers between devices: 192 us -> 0 us
  Pallas kernels: 0 us -> 107 us
  local copies, waits for them, and re-layouts: 109 us -> 6.75 us
  other arithmetic: 32.9 us -> 9.36 us
  starting transfers between devices: 18 us -> 0 us
    all_to_all x2 -> x0, waiting for transfers between devices: 192 us -> none  [the longest x1 98.8 us: relocate(): lax.all_to_all(outgoing, 'rows', split_axis=1, concat_axis=0, tiled=True)]
    pallas_call x0 -> x1, Pallas kernels: none -> 107 us  [relocate(): pl.pallas_call(functools.partial(relocate_kernel, devices, heads), out_sh...]
    reshape x4 -> x0, local copies, waits for them, and re-layouts: 28.1 us -> none  [the longest x1 8.6 us: unpacked_rows(): buffer[:, :, :state_size]]
    all_to_all x2 -> x0, starting transfers between devices: 18 us -> none  [the longest x1 12.2 us: relocate(): lax.all_to_all(outgoing, 'rows', split_axis=1, concat_axis=0, tiled=True)]
    all_to_all x2 -> x0, local copies, waits for them, and re-layouts: 15.1 us -> none  [the longest x1 8.9 us: relocate(): lax.all_to_all(back, 'rows', split_axis=0, concat_axis=2, tiled=True)]
    transpose x2 -> x0, local copies, waits for them, and re-layouts: 15.1 us -> none  [the longest x1 8.53 us: unpacked_rows(): jnp.transpose(state_part, (0, 2, 1, 3, 4))]
    concatenate x1 -> x0, local copies, waits for them, and re-layouts: 14.6 us -> none  [packed_rows(): return jnp.concatenate([state_part, tail_part, bc_part], axis=2)]
    gather x2 -> x0, local copies, waits for them, and re-layouts: 13.8 us -> none  [relocate(): jnp.take(spread, source, axis=0)]
  transfers between devices with their start and end apart: 2 -> 0, of which waited for: 2 -> 0; matrix products, arithmetic and copies ran while one was open for 2% -> 0% of each run, Pallas kernels for 0% -> 0%
where the time goes in v1:
time: 135 us; the launch traced here: 134 us
  Pallas kernels  107 us (79%)
  blocking collectives  10.5 us (8%)
  other arithmetic  9.36 us (7%)
  local copies, waits for them, and re-layouts  6.75 us (5%)
    pallas_call x1, Pallas kernels, relocate(): pl.pallas_call(functools.partial(relocate_kernel, devices, heads), out_sh...  107 us
    psum x1, blocking collectives, on_device(): lax.psum(jnp.sum(jnp.square(gated).reshape(slot_count, depth_dev, groups,...  10.5 us
    reduce_sum x1, other arithmetic, on_device(): readout = jnp.sum(candidate * expand_c[:, None], axis=-1) + skip_d * conv_x  4.42 us

profile of v1, /device:TPU:24, one launch (start us, length us, event | category | flops | bytes accessed | tf_op | source)
XLA Modules:
  0.0 134.2 jit_solution(14023906638891162543)
XLA Ops:
  0.7 0.7 clamp_compare_fusion
  1.4 0.7 broadcast_compare_fusion
  2.1 0.7 exp.101
  2.7 0.7 multiply_exponential_fusion.1
  3.5 0.7 slice_bitcast_fusion.11
  4.2 0.7 slice_bitcast_fusion.10
  4.9 0.7 slice_bitcast_fusion.5
  5.7 0.7 slice_bitcast_fusion.3
  6.4 0.7 copy-done
  7.1 0.7 copy-done.1
  7.9 0.7 copy-done.2
  8.5 106.8 %shard_map.192 = (f32[64,32,256]{2,1,0:T(8,128)S(1)}, f32[96,128]{1,0:T(8,128)S(1)}) custom-call(s32[128]{0:T(128)S(1)} %copy-done.2, f32[2,64,32,256]{3,2,1,0:T(8,128)} %bitcast.115, bf16[2,3,16,128]{3,2,1,0:T(8,128)(2,1)S(1)} %copy-done, bf16[2,3,2,4,256]{4,3,2,1,0:T(4,128)(2,1)S(1)} %copy-done.1), custom_call_target="tpu_custom_call" | custom-call | tf_op jit(solution)/shard_map/pallas_call | solution.py:168
  115.3 0.1 select_select_fusion.1
  115.4 0.1 maximum_select_fusion.1
  115.5 0.1 multiply_reduce_fusion.4
  115.7 0.7 maximum_select_fusion.3
  116.4 0.1 select_select_fusion.2
  116.4 0.1 maximum_select_fusion
  116.6 0.7 maximum_select_fusion.2
  117.4 0.4 slice_bitcast_fusion.1
  117.9 4.4 %multiply_reduce_fusion.1 = (f32[2,16,128]{2,1,0:T(8,128)S(1)}, f32[2,16,128]{2,1,0:T(8,128)S(1)}, f32[2,16,128,256]{3,2,1,0:T(8,128)}) fusion(f32[2,128,256]{2,1,0:T(8,128)S(1)} %bitcast.119, f32[2,128,256]{2,1,0:T(8,128)S(1)} %bitcast.118, f32[2,16,128]{2,1,0:T(8,128)S(1)} %get-tuple-element.41, f32[2,128]{1,0:T(2,128)S(1)} %get-tuple-element.18, ...), kind=kLoop, calls=%fused_computation.1 | loop fusion | flops 14671872 | bytes 11601926 | tf_op jit(solution)/shard_map/reduce_sum | solution.py:258
  122.4 0.1 reduce_sum.102
  122.4 0.1 reduce_sum.103
  122.5 0.1 reduce_sum.108
  122.6 0.1 reduce_sum.109
  122.7 10.5 %all-reduce = (f32[2,4]{1,0:T(2,128)S(1)}, f32[2,4]{1,0:T(2,128)S(1)}) all-reduce(f32[2,4]{1,0:T(2,128)S(1)} %reduce_sum.109, f32[2,4]{1,0:T(2,128)S(1)} %reduce_sum.103), channel_id=1, replica_groups=mesh['rows'=64,'tp'=4] {'tp'}, use_global_device_ids=true, to_apply=%region_11.12 | all-reduce | flops 16 | bytes 128 | tf_op jit(solution)/shard_map/psum | solution.py:260
  133.2 0.1 broadcast_in_dim.258
  133.3 0.1 mul.338
  133.3 0.1 broadcast_in_dim.261
  133.4 0.1 mul.353
  133.5 0.1 fusion.33
  133.6 0.6 pad_maximum_fusion
  (36 shorter events, 0.3 us)
Async XLA Ops:
  0.6 116.6 %copy-start.4 = (f32[16,128]{1,0:T(8,128)S(1)}, f32[16,128]{1,0:T(8,128)}, u32[]{:S(2)}) copy-start(f32[16,128]{1,0:T(8,128)} %param.27) | copy-start | bytes 24580
  0.6 114.9 %copy-start.9 = (f32[2,4,256]{2,1,0:T(4,128)S(1)}, f32[2,4,256]{2,1,0:T(4,128)}, u32[]{:S(2)}) copy-start(f32[2,4,256]{2,1,0:T(4,128)} %param.29) | copy-start | bytes 24580
  0.7 114.9 %copy-start.6 = (f32[4,2,4,256]{3,2,1,0:T(4,128)S(1)}, f32[4,2,4,256]{3,2,1,0:T(4,128)}, u32[]{:S(2)}) copy-start(f32[4,2,4,256]{3,2,1,0:T(4,128)} %param.28) | copy-start | bytes 98308
  0.7 115.9 %copy-start.7 = (f32[4,16,128]{2,1,0:T(8,128)S(1)}, f32[4,16,128]{2,1,0:T(8,128)}, u32[]{:S(2)}) copy-start(f32[4,16,128]{2,1,0:T(8,128)} %param.26) | copy-start | bytes 98308
  6.4 0.7 copy-start
  7.1 0.7 copy-start.1
  7.9 0.7 copy-start.2
  8.5 108.9 %copy-start.3 = (f32[2,16,128,256]{3,2,1,0:T(8,128)S(1)}, f32[2,16,128,256]{3,2,1,0:T(8,128)}, u32[]{:S(2)}) copy-start(f32[2,16,128,256]{3,2,1,0:T(8,128)} %param.17) | copy-start | bytes 12582916
  117.8 4.5 %copy-start.5 = (bf16[2,2,16,128]{3,2,1,0:T(8,128)(2,1)S(1)}, bf16[2,2,16,128]{3,2,1,0:T(8,128)(2,1)}, u32[]{:S(2)}) copy-start(bf16[2,2,16,128]{3,2,1,0:T(8,128)(2,1)} %param.23) | copy-start | bytes 49156
  117.9 4.4 %copy-start.10 = (f32[128]{0:T(128)S(1)}, f32[128]{0:T(128)}, u32[]{:S(2)}) copy-start(f32[128]{0:T(128)} %param.32) | copy-start | bytes 1540
  117.9 15.6 %copy-start.8 = (f32[16,128]{1,0:T(8,128)S(1)}, f32[16,128]{1,0:T(8,128)}, u32[]{:S(2)}) copy-start(f32[16,128]{1,0:T(8,128)} %param.33) | copy-start | bytes 24580

commit v2 on v1

v2 whole, which is shorter than its diff:
```python
import functools
import jax
import jax.numpy as jnp
from jax import lax
from jax.experimental import pallas as pl
from jax.experimental.pallas import tpu as pltpu
from jax.sharding import PartitionSpec as P

STEPS = 2
EPSILON = 1e-05
MESH = pl.DeviceIdType.MESH
CHUNKS = 2
TAIL_ROWS = 2
LANES = 128
DEPTH = 16
GROUPS = 4
PER_GROUP = 32
PART = PER_GROUP // CHUNKS
TP = 4

COEF = 0
INPUT_B = 256
Y_ROWS = 288
TAIL_X = 352
TAIL_BC = 448
PACK_ROWS = 544


def silu(v):
    return v / (1.0 + jnp.exp(-v))


def partner_of(me, i, devices):
    return lax.rem(me + i, devices)


def given_of(low, high, me):
    return jnp.where((low != 2 * me) & (high != 2 * me), 0, 1)


def relocate_kernel(
    devices,
    source_hbm,
    active_hbm,
    state_hbm,
    tail_x_hbm,
    tail_bc_hbm,
    x_new_hbm,
    z_new_hbm,
    bc_new_hbm,
    dt_new_hbm,
    conv_wx_hbm,
    conv_bx_hbm,
    conv_wbc_hbm,
    conv_bbc_hbm,
    dt_bias_hbm,
    a_log_hbm,
    skip_d_hbm,
    norm_gain_hbm,
    moved_a,
    moved_b,
    pack_hbm,
    source,
    active,
    state,
    tail_x,
    tail_bc,
    x_new,
    z_new,
    bc_new,
    dt_new,
    conv_wx,
    conv_bx,
    conv_wbc,
    conv_bbc,
    dt_bias,
    a_log,
    skip_d,
    norm_gain,
    tails,
    first_a,
    first_b,
    spread_a,
    spread_b,
    second_a,
    second_b,
    back_a,
    back_b,
    pack,
    rows_c,
    decays,
    extras,
    gates,
    dots,
    turned,
    sums,
    sums_in,
    load_sem,
    send_sem,
    recv_sem,
    sum_send_sem,
    sum_recv_sem,
    out_sem,
):
    me = lax.axis_index("rows")
    column = lax.axis_index("tp")
    first, spread, second, back = (
        (first_a, first_b),
        (spread_a, spread_b),
        (second_a, second_b),
        (back_a, back_b),
    )
    loads = [
        pltpu.make_async_copy(src, dst, load_sem.at[i])
        for i, (src, dst) in enumerate(
            (
                (source_hbm, source),
                (tail_x_hbm, tail_x),
                (tail_bc_hbm, tail_bc),
                (state_hbm, state),
                (active_hbm, active),
                (x_new_hbm, x_new),
                (z_new_hbm, z_new),
                (bc_new_hbm, bc_new),
                (dt_new_hbm, dt_new),
                (conv_wx_hbm, conv_wx),
                (conv_bx_hbm, conv_bx),
                (conv_wbc_hbm, conv_wbc),
                (conv_bbc_hbm, conv_bbc),
                (dt_bias_hbm, dt_bias),
                (a_log_hbm, a_log),
                (skip_d_hbm, skip_d),
                (norm_gain_hbm, norm_gain),
            )
        )
    ]
    for load in loads:
        load.start()
    barrier = pltpu.get_barrier_semaphore()

    def greet(i, carry):
        pl.semaphore_signal(
            barrier,
            inc=1,
            device_id={"rows": partner_of(me, i, devices)},
            device_id_type=MESH,
        )
        return carry

    lax.fori_loop(1, devices, greet, 0)
    for j in range(1, TP):
        pl.semaphore_signal(
            barrier,
            inc=1,
            device_id={"tp": lax.rem(column + j, TP)},
            device_id_type=MESH,
        )

    loads[0].wait()
    low = source[2 * me]
    high = source[2 * me + 1]
    given = given_of(low, high, me)
    kept = 1 - given
    kept_slot = jnp.where(low == 2 * me + kept, 0, 1)
    moved_slot = 1 - kept_slot

    loads[1].wait()
    loads[2].wait()
    for k in range(3):
        tails[DEPTH * k : DEPTH * (k + 1), :] = tail_x[given, k].astype(jnp.float32)
        for b in range(2):
            entry = tail_bc[given, k, b].astype(jnp.float32)
            at = 48 + (2 * k + b) * 8
            tails[at : at + 4, :] = entry[:, :LANES]
            tails[at + 4 : at + 8, :] = entry[:, LANES:]

    def remote(phase, chunk, to):
        source_ref, target_ref = ((first, spread), (second, back))[phase]
        return pltpu.make_async_remote_copy(
            src_ref=source_ref[chunk].at[to],
            dst_ref=target_ref[chunk].at[me],
            send_sem=send_sem.at[phase, chunk],
            recv_sem=recv_sem.at[phase, chunk],
            device_id={"rows": to},
            device_id_type=MESH,
        )

    def all_pieces(phase, chunk):
        source_ref, target_ref = ((first, spread), (second, back))[phase]
        return pltpu.make_async_remote_copy(
            src_ref=source_ref[chunk].at[pl.ds(0, devices - 1)],
            dst_ref=target_ref[chunk].at[pl.ds(0, devices - 1)],
            send_sem=send_sem.at[phase, chunk],
            recv_sem=recv_sem.at[phase, chunk],
            device_id={"rows": partner_of(me, 1, devices)},
            device_id_type=MESH,
        )

    def fill(chunk, piece, into, at):
        rows = state[given, piece, chunk * PART : (chunk + 1) * PART, :]
        into[at, 0:PART, :] = rows[:, :LANES]
        into[at, PART : 2 * PART, :] = rows[:, LANES:]
        if chunk == 0:
            into[at, 2 * PART, :] = tails[piece, :]
            into[at, 2 * PART + 1, :] = tails[64 + lax.rem(piece, 32), :]

    loads[3].wait()
    pl.semaphore_wait(barrier, devices - 1 + TP - 1)
    for chunk in range(CHUNKS):

        def begin(i, carry, chunk=chunk):
            to = partner_of(me, i, devices)
            fill(chunk, to, first[chunk], to)
            remote(0, chunk, to).start()
            return carry

        lax.fori_loop(1, devices, begin, 0)
        fill(chunk, me, spread[chunk], me)

    for load in loads[4:]:
        load.wait()
    group_of_lane = lax.broadcasted_iota(jnp.int32, (GROUPS, LANES), 1) // PER_GROUP
    own_group = group_of_lane == lax.broadcasted_iota(jnp.int32, (GROUPS, LANES), 0)
    lane = lax.broadcasted_iota(jnp.int32, (8, LANES), 1)

    def by_head(values):
        return jnp.sum(jnp.where(own_group, values, 0.0), axis=0, keepdims=True)

    def prepare(row, slot, window_x, window_bc):
        live = active[slot] == 1
        new_x = [x_new[s, slot].astype(jnp.float32) for s in range(STEPS)]
        new_bc = [
            [bc_new[s, slot, b].astype(jnp.float32) for b in range(2)] for s in range(STEPS)
        ]
        frames_x = window_x + new_x
        frames_bc = window_bc + new_bc
        conv_x = []
        conv_b = []
        conv_c = []
        sizes = []
        decay = []
        rate = jnp.exp(a_log[...])
        for s in range(STEPS):
            total = frames_x[s] * conv_wx[0]
            for k in range(1, 4):
                total = total + frames_x[s + k] * conv_wx[k]
            conv_x.append(silu(total + conv_bx[...]))
            pair = []
            for b in range(2):
                total = frames_bc[s][b] * conv_wbc[0, b]
                for k in range(1, 4):
                    total = total + frames_bc[s + k][b] * conv_wbc[k, b]
                pair.append(silu(total + conv_bbc[b]))
            conv_b.append(pair[0])
            conv_c.append(pair[1])
            raw = jnp.where(slot == 0, dt_new[s, 0:1, :], dt_new[s, 1:2, :]) + dt_bias[...]
            size = jnp.maximum(raw, 0.0) + jnp.log1p(jnp.exp(-jnp.abs(raw)))
            sizes.append(size)
            decay.append(jnp.exp(-size * rate))
            for half in range(2):
                for g in range(GROUPS):
                    rows_c[row, s, half, g] = jnp.broadcast_to(
                        pair[1][g : g + 1, half * LANES : (half + 1) * LANES], (8, LANES)
                    )
            at = INPUT_B + (row * STEPS + s) * 8
            pack[at : at + 4, :] = pair[0][:, :LANES]
            pack[at + 4 : at + 8, :] = pair[0][:, LANES:]
            gates[row, s] = silu(z_new[s, slot].astype(jnp.float32))

        def overlap(i, j):
            return by_head(jnp.sum(conv_b[i] * conv_c[j], axis=1, keepdims=True))

        skip = skip_d[...]
        put_in = [sizes[s] * conv_x[s] for s in range(STEPS)]
        carried = put_in[0] * decay[1]
        both = decay[0] * decay[1]
        decays[row, 0] = jnp.broadcast_to(decay[0], (DEPTH, LANES))
        decays[row, 1] = jnp.broadcast_to(both, (DEPTH, LANES))
        extras[row, 0] = put_in[0] * overlap(0, 0) + skip * conv_x[0]
        extras[row, 1] = (
            carried * overlap(0, 1) + put_in[1] * overlap(1, 1) + skip * conv_x[1]
        )
        turned[0:DEPTH, :] = jnp.where(live, carried, 0.0)
        turned[DEPTH : 2 * DEPTH, :] = jnp.where(live, put_in[1], 0.0)
        turned[2 * DEPTH : 2 * DEPTH + 8, :] = jnp.broadcast_to(
            jnp.where(live, both, 1.0), (8, LANES)
        )
        turned[2 * DEPTH + 8 :, :] = jnp.zeros((LANES - 2 * DEPTH - 8, LANES), jnp.float32)
        at = COEF + row * LANES
        pack[at : at + LANES, :] = jnp.transpose(turned[...])
        for k in range(3):
            at = TAIL_X + (row * 3 + k) * DEPTH
            pack[at : at + DEPTH, :] = jnp.where(live, frames_x[k + 2], frames_x[k])
            for b in range(2):
                entry = jnp.where(live, frames_bc[k + 2][b], frames_bc[k][b])
                at = TAIL_BC + ((row * 3 + k) * 2 + b) * 8
                pack[at : at + 4, :] = entry[:, :LANES]
                pack[at + 4 : at + 8, :] = entry[:, LANES:]

    def readout(row, octets, piece):
        def one_group(g, carry):
            c = [
                [rows_c[row, s, half, g] for half in range(2)] for s in range(STEPS)
            ]
            for octet in octets:
                held = [jnp.zeros((8, LANES), jnp.float32) for _ in range(STEPS)]
                for p in range(DEPTH):
                    left, right = piece(GROUPS * p + g, octet)
                    for s in range(STEPS):
                        dot = jnp.sum(
                            left * c[s][0] + right * c[s][1], axis=1, keepdims=True
                        )
                        held[s] = jnp.where(lane == p, dot, held[s])
                for s in range(STEPS):
                    at = pl.multiple_of(g * PER_GROUP + octet * 8, 8)
                    dots[s, pl.ds(at, 8), :] = held[s]
            return carry

        lax.fori_loop(0, GROUPS, one_group, 0)

    def finish(row):
        for s in range(STEPS):
            dot = jnp.transpose(dots[s])[0:DEPTH, :]
            gated = (decays[row, s] * dot + extras[row, s]) * gates[row, s]
            gates[row, s] = gated
            sums[row * STEPS + s : row * STEPS + s + 1, :] = jnp.sum(
                gated * gated, axis=0, keepdims=True
            )

    prepare(
        0,
        kept_slot,
        [tail_x[kept, k].astype(jnp.float32) for k in range(3)],
        [[tail_bc[kept, k, b].astype(jnp.float32) for b in range(2)] for k in range(3)],
    )
    sums[4:8, :] = jnp.zeros((4, LANES), jnp.float32)

    def kept_piece(at, octet):
        rows = state[kept, at, 8 * octet : 8 * octet + 8, :]
        return rows[:, :LANES], rows[:, LANES:]

    readout(0, range(PER_GROUP // 8), kept_piece)
    finish(0)

    def giver(to):
        from_low = lax.shift_right_logical(source[2 * to], 1)
        from_high = lax.shift_right_logical(source[2 * to + 1], 1)
        return jnp.where(from_low != to, from_low, from_high)

    for chunk in range(CHUNKS):
        all_pieces(0, chunk).wait_recv()

        def forward(i, carry, chunk=chunk):
            to = partner_of(me, i, devices)
            second[chunk][to] = spread[chunk][giver(to)]
            remote(1, chunk, to).start()
            return carry

        lax.fori_loop(1, devices, forward, 0)
        back[chunk][me] = spread[chunk][giver(me)]

    outs = [
        pltpu.make_async_copy(back_a, moved_a, out_sem.at[0]),
        pltpu.make_async_copy(back_b, moved_b, out_sem.at[1]),
        pltpu.make_async_copy(pack, pack_hbm, out_sem.at[2]),
    ]
    for chunk in range(CHUNKS):
        all_pieces(1, chunk).wait_recv()
        outs[chunk].start()
        if chunk == 0:

            def untail(k, carry):
                tails[64 + lax.rem(k, 32), :] = back_a[k, 2 * PART + 1, :]
                tails[k, :] = back_a[k, 2 * PART, :]
                return carry

            lax.fori_loop(0, devices, untail, 0)
            window_bc = [
                [
                    jnp.concatenate(
                        [
                            tails[48 + (2 * k + b) * 8 : 52 + (2 * k + b) * 8, :],
                            tails[52 + (2 * k + b) * 8 : 56 + (2 * k + b) * 8, :],
                        ],
                        axis=1,
                    )
                    for b in range(2)
                ]
                for k in range(3)
            ]
            prepare(
                1,
                moved_slot,
                [tails[DEPTH * k : DEPTH * (k + 1), :] for k in range(3)],
                window_bc,
            )

        def moved_piece(at, octet, chunk=chunk):
            within = 8 * octet - PART * chunk
            return (
                back[chunk][at, within : within + 8, :],
                back[chunk][at, PART + within : PART + within + 8, :],
            )

        readout(1, range(chunk * PART // 8, (chunk + 1) * PART // 8), moved_piece)
    finish(1)

    exchanges = [
        pltpu.make_async_remote_copy(
            src_ref=sums,
            dst_ref=sums_in.at[j - 1],
            send_sem=sum_send_sem.at[j - 1],
            recv_sem=sum_recv_sem.at[j - 1],
            device_id={"tp": lax.rem(column + j, TP)},
            device_id_type=MESH,
        )
        for j in range(1, TP)
    ]
    for exchange in exchanges:
        exchange.start()
    same_group = (
        lax.broadcasted_iota(jnp.int32, (LANES, LANES), 0) // PER_GROUP
        == lax.broadcasted_iota(jnp.int32, (LANES, LANES), 1) // PER_GROUP
    ).astype(jnp.float32)
    for exchange in exchanges:
        exchange.wait_recv()
    totals = jnp.dot(
        sums[...] + sums_in[0] + sums_in[1] + sums_in[2],
        same_group,
        preferred_element_type=jnp.float32,
        precision=lax.Precision.HIGHEST,
    )
    factor = lax.rsqrt(totals / (DEPTH * TP * PER_GROUP) + EPSILON)
    for row in range(2):
        live = active[jnp.where(row == 0, kept_slot, moved_slot)] == 1
        for s in range(STEPS):
            scale = factor[row * STEPS + s : row * STEPS + s + 1, :]
            at = Y_ROWS + (row * STEPS + s) * DEPTH
            pack[at : at + DEPTH, :] = jnp.where(
                live, gates[row, s] * scale * norm_gain[...], 0.0
            )
    outs[2].start()
    for exchange in exchanges:
        exchange.wait_send()
    for phase in range(2):
        for chunk in range(CHUNKS):
            all_pieces(phase, chunk).wait_send()
    for out in outs:
        out.wait()


QUARTERS = 4


def state_kernel(
    devices,
    source_hbm,
    state_hbm,
    moved_a_hbm,
    moved_b_hbm,
    pack_hbm,
    state_out,
    tail_x_out,
    tail_bc_out,
    y_out,
    source,
    kept_in,
    moved_a,
    moved_b,
    pack,
    result,
    tail_x,
    tail_bc,
    y,
    sem,
    part_sem,
):
    me = lax.axis_index("rows")
    size = devices // QUARTERS

    def piece_range(q):
        return pl.ds(q * size, size)

    source_load = pltpu.make_async_copy(source_hbm, source, sem.at[0])
    pack_load = pltpu.make_async_copy(pack_hbm, pack, sem.at[1])
    source_load.start()
    pack_load.start()
    moved_loads = [
        [
            pltpu.make_async_copy(
                hbm.at[piece_range(q)], vmem.at[piece_range(q)], part_sem.at[c, q]
            )
            for c, (hbm, vmem) in enumerate(((moved_a_hbm, moved_a), (moved_b_hbm, moved_b)))
        ]
        for q in range(QUARTERS)
    ]
    for pair in moved_loads:
        for load in pair:
            load.start()
    source_load.wait()
    low = source[2 * me]
    high = source[2 * me + 1]
    kept = 1 - given_of(low, high, me)
    kept_slot = jnp.where(low == 2 * me + kept, 0, 1)
    slots = (kept_slot, 1 - kept_slot)
    kept_loads = [
        pltpu.make_async_copy(
            state_hbm.at[kept, piece_range(q)], kept_in.at[piece_range(q)], part_sem.at[2, q]
        )
        for q in range(QUARTERS)
    ]
    for load in kept_loads:
        load.start()
    pack_load.wait()
    writes = []
    for row in (1, 0):
        base = COEF + row * LANES
        b = [
            pack[
                INPUT_B + (row * STEPS + s) * 8 : INPUT_B + (row * STEPS + s) * 8 + 8, :
            ]
            for s in range(STEPS)
        ]
        for q in range(QUARTERS):
            if row == 1:
                for load in moved_loads[q]:
                    load.wait()
            else:
                kept_loads[q].wait()
            for p in range(q * DEPTH // QUARTERS, (q + 1) * DEPTH // QUARTERS):
                for g in range(GROUPS):
                    k = GROUPS * p + g
                    for octet in range(PER_GROUP // 8):
                        head = base + g * PER_GROUP + octet * 8
                        u1 = pack[head : head + 8, p : p + 1]
                        u2 = pack[head : head + 8, DEPTH + p : DEPTH + p + 1]
                        decay = pack[head : head + 8, 2 * DEPTH : 2 * DEPTH + 1]
                        for half in range(2):
                            if row == 1:
                                chunk = octet * 8 // PART
                                at = half * PART + octet * 8 - chunk * PART
                                held = (moved_a, moved_b)[chunk][k, at : at + 8, :]
                            else:
                                held = kept_in[
                                    k,
                                    octet * 8 : octet * 8 + 8,
                                    half * LANES : (half + 1) * LANES,
                                ]
                            at = half * GROUPS + g
                            result[
                                row,
                                k,
                                octet * 8 : octet * 8 + 8,
                                half * LANES : (half + 1) * LANES,
                            ] = (
                                held * decay + u1 * b[0][at : at + 1, :] + u2 * b[1][at : at + 1, :]
                            )
            write = pltpu.make_async_copy(
                result.at[row, piece_range(q)],
                state_out.at[slots[row], piece_range(q)],
                part_sem.at[3 + row, q],
            )
            write.start()
            writes.append(write)
        slot = slots[row]
        for s in range(STEPS):
            at = Y_ROWS + (row * STEPS + s) * DEPTH
            y[s, slot] = pack[at : at + DEPTH, :].astype(jnp.bfloat16)
        for k in range(3):
            at = TAIL_X + (row * 3 + k) * DEPTH
            tail_x[slot, k] = pack[at : at + DEPTH, :].astype(jnp.bfloat16)
            for c in range(2):
                at = TAIL_BC + ((row * 3 + k) * 2 + c) * 8
                tail_bc[slot, k, c] = jnp.concatenate(
                    [pack[at : at + 4, :], pack[at + 4 : at + 8, :]], axis=1
                ).astype(jnp.bfloat16)
    for i, (vmem, hbm) in enumerate(((tail_x, tail_x_out), (tail_bc, tail_bc_out), (y, y_out))):
        write = pltpu.make_async_copy(vmem, hbm, sem.at[2 + i])
        write.start()
        writes.append(write)
    for write in writes:
        write.wait()


def on_device(
    state_in,
    tail_x,
    tail_bc,
    source,
    active,
    x_new,
    z_new,
    bc_new,
    dt_new,
    conv_wx,
    conv_bx,
    conv_wbc,
    conv_bbc,
    dt_bias,
    a_log,
    skip_d,
    norm_gain,
):
    devices = lax.axis_size("rows")
    slots, depth, head_count, width = state_in.shape
    pieces = state_in.reshape(slots, devices, PER_GROUP, width)
    operands = (
        source,
        active,
        pieces,
        tail_x,
        tail_bc,
        x_new,
        z_new,
        bc_new,
        dt_new,
        conv_wx,
        conv_bx,
        conv_wbc,
        conv_bbc,
        dt_bias.reshape(1, -1),
        a_log.reshape(1, -1),
        skip_d.reshape(1, -1),
        norm_gain,
    )
    long_buffer = pltpu.VMEM((devices, 2 * PART + TAIL_ROWS, LANES), jnp.float32)
    short_buffer = pltpu.VMEM((devices, 2 * PART, LANES), jnp.float32)
    hbm = pl.BlockSpec(memory_space=pltpu.HBM)
    moved_a, moved_b, pack = pl.pallas_call(
        functools.partial(relocate_kernel, devices),
        out_shape=(
            jax.ShapeDtypeStruct(long_buffer.shape, jnp.float32),
            jax.ShapeDtypeStruct(short_buffer.shape, jnp.float32),
            jax.ShapeDtypeStruct((PACK_ROWS, LANES), jnp.float32),
        ),
        in_specs=[hbm] * len(operands),
        out_specs=(hbm, hbm, hbm),
        scratch_shapes=[
            pltpu.SMEM(source.shape, jnp.int32),
            pltpu.SMEM(active.shape, jnp.int32),
        ]
        + [pltpu.VMEM(a.shape, a.dtype) for a in operands[2:]]
        + [pltpu.VMEM((96, LANES), jnp.float32)]
        + [long_buffer, short_buffer] * 4
        + [
            pltpu.VMEM((PACK_ROWS, LANES), jnp.float32),
            pltpu.VMEM((2, STEPS, 2, GROUPS, 8, LANES), jnp.float32),
            pltpu.VMEM((2, STEPS, DEPTH, LANES), jnp.float32),
            pltpu.VMEM((2, STEPS, DEPTH, LANES), jnp.float32),
            pltpu.VMEM((2, STEPS, DEPTH, LANES), jnp.float32),
            pltpu.VMEM((STEPS, LANES, LANES), jnp.float32),
            pltpu.VMEM((LANES, LANES), jnp.float32),
            pltpu.VMEM((8, LANES), jnp.float32),
            pltpu.VMEM((TP - 1, 8, LANES), jnp.float32),
            pltpu.SemaphoreType.DMA((len(operands),)),
            pltpu.SemaphoreType.DMA((2, CHUNKS)),
            pltpu.SemaphoreType.DMA((2, CHUNKS)),
            pltpu.SemaphoreType.DMA((TP - 1,)),
            pltpu.SemaphoreType.DMA((TP - 1,)),
            pltpu.SemaphoreType.DMA((3,)),
        ],
        compiler_params=pltpu.CompilerParams(
            collective_id=0, has_side_effects=True, vmem_limit_bytes=48 * 1024 * 1024
        ),
    )(*operands)
    state, window_x, window_bc, y = pl.pallas_call(
        functools.partial(state_kernel, devices),
        out_shape=(
            jax.ShapeDtypeStruct(pieces.shape, jnp.float32),
            jax.ShapeDtypeStruct(tail_x.shape, tail_x.dtype),
            jax.ShapeDtypeStruct(tail_bc.shape, tail_bc.dtype),
            jax.ShapeDtypeStruct(x_new.shape, jnp.bfloat16),
        ),
        in_specs=[hbm] * 5,
        out_specs=(hbm,) * 4,
        scratch_shapes=[
            pltpu.SMEM(source.shape, jnp.int32),
            pltpu.VMEM((devices, PER_GROUP, width), jnp.float32),
            long_buffer,
            short_buffer,
            pltpu.VMEM((PACK_ROWS, LANES), jnp.float32),
            pltpu.VMEM(pieces.shape, jnp.float32),
            pltpu.VMEM(tail_x.shape, tail_x.dtype),
            pltpu.VMEM(tail_bc.shape, tail_bc.dtype),
            pltpu.VMEM(x_new.shape, jnp.bfloat16),
            pltpu.SemaphoreType.DMA((5,)),
            pltpu.SemaphoreType.DMA((5, QUARTERS)),
        ],
        compiler_params=pltpu.CompilerParams(vmem_limit_bytes=48 * 1024 * 1024),
    )(source, pieces, moved_a, moved_b, pack)
    return state.reshape(state_in.shape), window_x, window_bc, y


def solution(mesh):
    return jax.shard_map(
        on_device,
        mesh=mesh,
        in_specs=(
            P("rows", "tp", None, None),
            P("rows", None, "tp", None),
            P("rows", None, None, None, None),
            P(),
            P("rows"),
            P(None, "rows", "tp", None),
            P(None, "rows", "tp", None),
            P(None, "rows", None, None, None),
            P(None, "rows", None),
            P(None, "tp", None),
            P("tp", None),
            P(),
            P(),
            P(),
            P(),
            P(),
            P("tp", None),
        ),
        out_specs=(
            P("rows", "tp", None, None),
            P("rows", None, "tp", None),
            P("rows", None, None, None, None),
            P(None, "rows", "tp", None),
        ),
        check_vma=False,
    )
```

time: 135 us -> 129 us (0.956)
  blocking collectives: 10.5 us -> 0 us
  other arithmetic: 9.36 us -> 0 us
  Pallas kernels: 107 us -> 116 us
  local copies, waits for them, and re-layouts: 6.75 us -> 11.2 us
    psum x1 -> x0, blocking collectives: 10.5 us -> none  [on_device(): lax.psum(jnp.sum(jnp.square(gated).reshape(slot_count, depth_dev, groups,...]
    pallas_call x1 -> x2, Pallas kernels: 107 us -> 116 us  [the longest x1 112 us: on_device(): pl.pallas_call(functools.partial(relocate_kernel, devices), out_shape=(ja...]
    unnamed x22 -> x32, local copies, waits for them, and re-layouts: 2.16 us -> 11.2 us
    reduce_sum x6 -> x0, other arithmetic: 4.73 us -> none  [the longest x1 4.42 us: on_device(): readout = jnp.sum(candidate * expand_c[:, None], axis=-1) + skip_d * conv_x]
    broadcast_in_dim x9 -> x0, local copies, waits for them, and re-layouts: 2.12 us -> none  [the longest x3 1.9 us: pick(): jnp.where((safe == 0).reshape((2,) + (1,) * new.ndim), array[0][None], ar...]
    select_n x6 -> x0, other arithmetic: 1.71 us -> none  [the longest x2 0.78 us: on_device(): jnp.where(live_bc, jnp.concatenate([window_bc[:, 1:], entry_bc[:, None]],...]
    another operation x2 -> x0, local copies, waits for them, and re-layouts: 1.44 us -> none  [the longest x1 0.72 us: on_device(): entry_bc[:, None]]
    eq x2 -> x0, other arithmetic: 1.41 us -> none  [the longest x1 0.75 us: pick(): safe == 0]
where the time goes in v2:
time: 129 us; the launch traced here: 128 us
  Pallas kernels  116 us (90%)
  local copies, waits for them, and re-layouts  11.2 us (9%)
    pallas_call x1, Pallas kernels, on_device(): pl.pallas_call(functools.partial(relocate_kernel, devices), out_shape=(ja...  112 us
    unnamed x32, local copies, waits for them, and re-layouts  11.2 us
    pallas_call x1, Pallas kernels, on_device(): pl.pallas_call(functools.partial(state_kernel, devices), out_shape=(jax.S...  4.52 us

profile of v2, /device:TPU:24, one launch (start us, length us, event | category | flops | bytes accessed | tf_op | source)
XLA Modules:
  0.0 128.3 jit_solution(14638457984573100672)
XLA Ops:
  0.6 0.0 copy-start
  0.6 0.7 copy-done
  1.4 0.0 copy-start.1
  1.4 0.8 copy-done.1
  2.2 0.0 copy-start.2
  2.2 0.7 copy-done.2
  2.9 0.0 copy-start.3
  2.9 0.7 copy-done.3
  3.6 0.0 copy-start.4
  3.6 0.7 copy-done.4
  4.4 0.7 copy-done.5
  5.1 0.0 copy-start.6
  5.1 0.7 copy-done.6
  5.8 0.0 copy-start.7
  5.8 0.7 copy-done.7
  6.5 0.0 copy-start.8
  6.5 0.7 copy-done.8
  7.2 0.0 copy-start.9
  7.2 0.7 copy-done.9
  7.9 0.0 copy-start.10
  7.9 0.7 copy-done.10
  8.6 0.7 copy-done.11
  9.2 0.0 copy-start.12
  9.2 0.7 copy-done.12
  9.9 0.0 copy-start.13
  9.9 0.7 copy-done.13
  10.5 0.0 copy-start.14
  10.5 0.7 copy-done.14
  11.2 0.0 copy-start.15
  11.2 0.7 copy-done.15
  11.8 111.9 %shard_map.192 = (f32[64,34,128]{2,1,0:T(8,128)S(1)}, f32[64,32,128]{2,1,0:T(8,128)S(1)}, f32[544,128]{1,0:T(8,128)S(1)}) custom-call(s32[128]{0:T(128)S(1)} %copy-done.11, s32[2]{0:T(128)S(1)} %copy-done.12, f32[2,64,32,256]{3,2,1,0:T(8,128)} %bitcast.8, bf16[2,3,16,128]{3,2,1,0:T(8,128)(2,1)S(1)} %copy-done.2, bf16[2,3,2,4,256]{4,3,2,1,0:T(4,128)(2,1)S(1)} %copy-done.3, ...), custom_call_target="tpu_custom_call" | custom-call | tf_op jit(solution)/shard_map/pallas_call | solution.py:629
  123.7 4.5 %shard_map.193 = (f32[2,64,32,256]{3,2,1,0:T(8,128)}, bf16[2,3,16,128]{3,2,1,0:T(8,128)(2,1)}, bf16[2,3,2,4,256]{4,3,2,1,0:T(4,128)(2,1)}, bf16[2,2,16,128]{3,2,1,0:T(8,128)(2,1)}) custom-call(s32[128]{0:T(128)S(1)} %copy-done.11, f32[2,64,32,256]{3,2,1,0:T(8,128)} %bitcast.9, f32[64,34,128]{2,1,0:T(8,128)S(1)} %get-tuple-element.11.moved_a_hbm, ...), custom_call_target="tpu_custom_call" | custom-call | tf_op jit(solution)/shard_map/pallas_call | solution.py:666
  (2 shorter events, 0.0 us)
Async XLA Ops:
  0.6 0.8 copy-start
  1.4 0.8 copy-start.1
  2.2 0.7 copy-start.2
  2.9 0.7 copy-start.3
  3.6 0.7 copy-start.4
  4.3 0.7 copy-start.5
  5.1 0.7 copy-start.6
  5.8 0.7 copy-start.7
  6.5 0.7 copy-start.8
  7.2 0.7 copy-start.9
  7.9 0.7 copy-start.10
  8.6 0.7 copy-start.11
  9.2 0.7 copy-start.12
  9.9 0.7 copy-start.13
  10.5 0.7 copy-start.14
  11.2 0.7 copy-start.15

commit v3 on v2

--- a/solution.py
+++ b/solution.py
@@ -660,7 +660,7 @@
             pltpu.SemaphoreType.DMA((3,)),
         ],
         compiler_params=pltpu.CompilerParams(
-            collective_id=0, has_side_effects=True, vmem_limit_bytes=48 * 1024 * 1024
+            collective_id=0, has_side_effects=True, vmem_limit_bytes=60 * 1024 * 1024
         ),
     )(*operands)
     state, window_x, window_bc, y = pl.pallas_call(
@@ -686,7 +686,7 @@
             pltpu.SemaphoreType.DMA((5,)),
             pltpu.SemaphoreType.DMA((5, QUARTERS)),
         ],
-        compiler_params=pltpu.CompilerParams(vmem_limit_bytes=48 * 1024 * 1024),
+        compiler_params=pltpu.CompilerParams(vmem_limit_bytes=60 * 1024 * 1024),
     )(source, pieces, moved_a, moved_b, pack)
     return state.reshape(state_in.shape), window_x, window_bc, y
 

time: 129 us -> 119 us (0.922)
  local copies, waits for them, and re-layouts: 11.2 us -> 0 us
  Pallas kernels: 116 us -> 118 us
    unnamed x32 -> x0, local copies, waits for them, and re-layouts: 11.2 us -> none
where the time goes in v3:
time: 119 us
  Pallas kernels  118 us (99%)
    pallas_call x1, Pallas kernels, on_device(): pl.pallas_call(functools.partial(relocate_kernel, devices), out_shape=(ja...  112 us
    pallas_call x1, Pallas kernels, on_device(): pl.pallas_call(functools.partial(state_kernel, devices), out_shape=(jax.S...  5.49 us

profile of v3, /device:TPU:24, one launch (start us, length us, event | category | flops | bytes accessed | tf_op | source)
XLA Modules:
  0.0 118.6 jit_solution(125609575748125968)
XLA Ops:
  0.6 112.4 %shard_map.192 = (f32[64,34,128]{2,1,0:T(8,128)}, f32[64,32,128]{2,1,0:T(8,128)}, f32[544,128]{1,0:T(8,128)}) custom-call(s32[128]{0:T(128)} %source_hbm.3, s32[2]{0:T(128)} %active_hbm.1, f32[2,64,32,256]{3,2,1,0:T(8,128)} %bitcast.5, bf16[2,3,16,128]{3,2,1,0:T(8,128)(2,1)} %tail_x_hbm.1, bf16[2,3,2,4,256]{4,3,2,1,0:T(4,128)(2,1)} %tail_bc_hbm.1, ...), custom_call_target="tpu_custom_call" | custom-call | tf_op jit(solution)/shard_map/pallas_call | solution.py:629
  113.1 5.5 %shard_map.193 = (f32[2,64,32,256]{3,2,1,0:T(8,128)}, bf16[2,3,16,128]{3,2,1,0:T(8,128)(2,1)}, bf16[2,3,2,4,256]{4,3,2,1,0:T(4,128)(2,1)}, bf16[2,2,16,128]{3,2,1,0:T(8,128)(2,1)}) custom-call(s32[128]{0:T(128)} %source_hbm.3, f32[2,64,32,256]{3,2,1,0:T(8,128)} %bitcast.6, f32[64,34,128]{2,1,0:T(8,128)} %get-tuple-element.11.moved_a_hbm, ...), custom_call_target="tpu_custom_call" | custom-call | tf_op jit(solution)/shard_map/pallas_call | solution.py:666

commit v4 on v3

--- a/solution.py
+++ b/solution.py
@@ -18,12 +18,10 @@
 PART = PER_GROUP // CHUNKS
 TP = 4
 
-COEF = 0
-INPUT_B = 256
-Y_ROWS = 288
-TAIL_X = 352
-TAIL_BC = 448
-PACK_ROWS = 544
+Y_ROWS = 0
+TAIL_X = 64
+TAIL_BC = 160
+PACK_ROWS = 256
 
 
 def silu(v):
@@ -56,10 +54,9 @@
     dt_bias_hbm,
     a_log_hbm,
     skip_d_hbm,
-    norm_gain_hbm,
-    moved_a,
-    moved_b,
+    final_hbm,
     pack_hbm,
+    sums_hbm,
     source,
     active,
     state,
@@ -76,7 +73,6 @@
     dt_bias,
     a_log,
     skip_d,
-    norm_gain,
     tails,
     first_a,
     first_b,
@@ -87,14 +83,16 @@
     back_a,
     back_b,
     pack,
+    final,
+    rows_b,
     rows_c,
+    factors,
     decays,
     extras,
     gates,
     dots,
     turned,
     sums,
-    sums_in,
     load_sem,
     send_sem,
     recv_sem,
@@ -130,7 +128,6 @@
                 (dt_bias_hbm, dt_bias),
                 (a_log_hbm, a_log),
                 (skip_d_hbm, skip_d),
-                (norm_gain_hbm, norm_gain),
             )
         )
     ]
@@ -259,12 +256,9 @@
             decay.append(jnp.exp(-size * rate))
             for half in range(2):
                 for g in range(GROUPS):
-                    rows_c[row, s, half, g] = jnp.broadcast_to(
-                        pair[1][g : g + 1, half * LANES : (half + 1) * LANES], (8, LANES)
-                    )
-            at = INPUT_B + (row * STEPS + s) * 8
-            pack[at : at + 4, :] = pair[0][:, :LANES]
-            pack[at + 4 : at + 8, :] = pair[0][:, LANES:]
+                    at = slice(half * LANES, (half + 1) * LANES)
+                    rows_b[row, s, half, g] = jnp.broadcast_to(pair[0][g : g + 1, at], (8, LANES))
+                    rows_c[row, s, half, g] = jnp.broadcast_to(pair[1][g : g + 1, at], (8, LANES))
             gates[row, s] = silu(z_new[s, slot].astype(jnp.float32))
 
         def overlap(i, j):
@@ -286,8 +280,7 @@
             jnp.where(live, both, 1.0), (8, LANES)
         )
         turned[2 * DEPTH + 8 :, :] = jnp.zeros((LANES - 2 * DEPTH - 8, LANES), jnp.float32)
-        at = COEF + row * LANES
-        pack[at : at + LANES, :] = jnp.transpose(turned[...])
+        factors[row] = jnp.transpose(turned[...])
         for k in range(3):
             at = TAIL_X + (row * 3 + k) * DEPTH
             pack[at : at + DEPTH, :] = jnp.where(live, frames_x[k + 2], frames_x[k])
@@ -318,11 +311,37 @@
 
         lax.fori_loop(0, GROUPS, one_group, 0)
 
+    def update(row, octets, piece):
+        def one_group(g, carry):
+            b = [[rows_b[row, s, half, g] for half in range(2)] for s in range(STEPS)]
+            for octet in octets:
+                heads = pl.ds(pl.multiple_of(g * PER_GROUP + octet * 8, 8), 8)
+
+                def spread_out(at):
+                    return jnp.broadcast_to(factors[row, heads, at : at + 1], (8, LANES))
+
+                decay = spread_out(2 * DEPTH)
+                for p in range(DEPTH):
+                    u1 = spread_out(p)
+                    u2 = spread_out(DEPTH + p)
+                    k = GROUPS * p + g
+                    for half, held in enumerate(piece(k, octet)):
+                        final[
+                            row,
+                            k,
+                            8 * octet : 8 * octet + 8,
+                            half * LANES : (half + 1) * LANES,
+                        ] = held * decay + u1 * b[0][half] + u2 * b[1][half]
+            return carry
+
+        lax.fori_loop(0, GROUPS, one_group, 0)
+
     def finish(row):
         for s in range(STEPS):
             dot = jnp.transpose(dots[s])[0:DEPTH, :]
             gated = (decays[row, s] * dot + extras[row, s]) * gates[row, s]
-            gates[row, s] = gated
+            at = Y_ROWS + (row * STEPS + s) * DEPTH
+            pack[at : at + DEPTH, :] = gated
             sums[row * STEPS + s : row * STEPS + s + 1, :] = jnp.sum(
                 gated * gated, axis=0, keepdims=True
             )
@@ -341,6 +360,19 @@
 
     readout(0, range(PER_GROUP // 8), kept_piece)
     finish(0)
+    update(0, range(PER_GROUP // 8), kept_piece)
+    outs = [
+        pltpu.make_async_copy(final.at[0], final_hbm.at[0], out_sem.at[0]),
+        pltpu.make_async_copy(pack, pack_hbm, out_sem.at[1]),
+    ] + [
+        pltpu.make_async_copy(
+            final.at[1, :, pl.ds(chunk * PART, PART), :],
+            final_hbm.at[1, :, pl.ds(chunk * PART, PART), :],
+            out_sem.at[2 + chunk],
+        )
+        for chunk in range(CHUNKS)
+    ] + [pltpu.make_async_copy(sums, sums_hbm.at[0], out_sem.at[2 + CHUNKS])]
+    outs[0].start()
 
     def giver(to):
         from_low = lax.shift_right_logical(source[2 * to], 1)
@@ -359,14 +391,8 @@
         lax.fori_loop(1, devices, forward, 0)
         back[chunk][me] = spread[chunk][giver(me)]
 
-    outs = [
-        pltpu.make_async_copy(back_a, moved_a, out_sem.at[0]),
-        pltpu.make_async_copy(back_b, moved_b, out_sem.at[1]),
-        pltpu.make_async_copy(pack, pack_hbm, out_sem.at[2]),
-    ]
     for chunk in range(CHUNKS):
         all_pieces(1, chunk).wait_recv()
-        outs[chunk].start()
         if chunk == 0:
 
             def untail(k, carry):
@@ -402,13 +428,17 @@
                 back[chunk][at, PART + within : PART + within + 8, :],
             )
 
-        readout(1, range(chunk * PART // 8, (chunk + 1) * PART // 8), moved_piece)
+        octets = range(chunk * PART // 8, (chunk + 1) * PART // 8)
+        readout(1, octets, moved_piece)
+        if chunk < CHUNKS - 1:
+            update(1, octets, moved_piece)
+            outs[2 + chunk].start()
     finish(1)
 
     exchanges = [
         pltpu.make_async_remote_copy(
             src_ref=sums,
-            dst_ref=sums_in.at[j - 1],
+            dst_ref=sums_hbm.at[j],
             send_sem=sum_send_sem.at[j - 1],
             recv_sem=sum_recv_sem.at[j - 1],
             device_id={"tp": lax.rem(column + j, TP)},
@@ -418,28 +448,12 @@
     ]
     for exchange in exchanges:
         exchange.start()
-    same_group = (
-        lax.broadcasted_iota(jnp.int32, (LANES, LANES), 0) // PER_GROUP
-        == lax.broadcasted_iota(jnp.int32, (LANES, LANES), 1) // PER_GROUP
-    ).astype(jnp.float32)
+    for at in (1, 2 + CHUNKS):
+        outs[at].start()
+    update(1, octets, moved_piece)
+    outs[1 + CHUNKS].start()
     for exchange in exchanges:
         exchange.wait_recv()
-    totals = jnp.dot(
-        sums[...] + sums_in[0] + sums_in[1] + sums_in[2],
-        same_group,
-        preferred_element_type=jnp.float32,
-        precision=lax.Precision.HIGHEST,
-    )
-    factor = lax.rsqrt(totals / (DEPTH * TP * PER_GROUP) + EPSILON)
-    for row in range(2):
-        live = active[jnp.where(row == 0, kept_slot, moved_slot)] == 1
-        for s in range(STEPS):
-            scale = factor[row * STEPS + s : row * STEPS + s + 1, :]
-            at = Y_ROWS + (row * STEPS + s) * DEPTH
-            pack[at : at + DEPTH, :] = jnp.where(
-                live, gates[row, s] * scale * norm_gain[...], 0.0
-            )
-    outs[2].start()
     for exchange in exchanges:
         exchange.wait_send()
     for phase in range(2):
@@ -449,26 +463,27 @@
         out.wait()
 
 
-QUARTERS = 4
-
-
-def state_kernel(
+PARTS = 2
+
+
+def place_kernel(
     devices,
     source_hbm,
-    state_hbm,
-    moved_a_hbm,
-    moved_b_hbm,
+    active_hbm,
+    norm_gain_hbm,
+    sums_hbm,
+    final_hbm,
     pack_hbm,
     state_out,
     tail_x_out,
     tail_bc_out,
     y_out,
     source,
-    kept_in,
-    moved_a,
-    moved_b,
+    active,
+    norm_gain,
+    sums,
+    held,
     pack,
-    result,
     tail_x,
     tail_bc,
     y,
@@ -476,96 +491,69 @@
     part_sem,
 ):
     me = lax.axis_index("rows")
-    size = devices // QUARTERS
-
-    def piece_range(q):
-        return pl.ds(q * size, size)
-
+    size = devices // PARTS
     source_load = pltpu.make_async_copy(source_hbm, source, sem.at[0])
-    pack_load = pltpu.make_async_copy(pack_hbm, pack, sem.at[1])
+    small_loads = [
+        pltpu.make_async_copy(hbm, vmem, sem.at[1 + i])
+        for i, (hbm, vmem) in enumerate(
+            (
+                (sums_hbm, sums),
+                (pack_hbm, pack),
+                (active_hbm, active),
+                (norm_gain_hbm, norm_gain),
+            )
+        )
+    ]
     source_load.start()
-    pack_load.start()
-    moved_loads = [
-        [
-            pltpu.make_async_copy(
-                hbm.at[piece_range(q)], vmem.at[piece_range(q)], part_sem.at[c, q]
-            )
-            for c, (hbm, vmem) in enumerate(((moved_a_hbm, moved_a), (moved_b_hbm, moved_b)))
-        ]
-        for q in range(QUARTERS)
+    for load in small_loads:
+        load.start()
+    parts = [(row, q) for row in range(2) for q in range(PARTS)]
+    loads = [
+        pltpu.make_async_copy(
+            final_hbm.at[row, pl.ds(q * size, size)],
+            held.at[row, pl.ds(q * size, size)],
+            part_sem.at[row, q],
+        )
+        for row, q in parts
     ]
-    for pair in moved_loads:
-        for load in pair:
-            load.start()
+    for load in loads:
+        load.start()
     source_load.wait()
     low = source[2 * me]
     high = source[2 * me + 1]
     kept = 1 - given_of(low, high, me)
     kept_slot = jnp.where(low == 2 * me + kept, 0, 1)
     slots = (kept_slot, 1 - kept_slot)
-    kept_loads = [
-        pltpu.make_async_copy(
-            state_hbm.at[kept, piece_range(q)], kept_in.at[piece_range(q)], part_sem.at[2, q]
-        )
-        for q in range(QUARTERS)
-    ]
-    for load in kept_loads:
-        load.start()
-    pack_load.wait()
     writes = []
-    for row in (1, 0):
-        base = COEF + row * LANES
-        b = [
-            pack[
-                INPUT_B + (row * STEPS + s) * 8 : INPUT_B + (row * STEPS + s) * 8 + 8, :
-            ]
-            for s in range(STEPS)
-        ]
-        for q in range(QUARTERS):
-            if row == 1:
-                for load in moved_loads[q]:
-                    load.wait()
-            else:
-                kept_loads[q].wait()
-            for p in range(q * DEPTH // QUARTERS, (q + 1) * DEPTH // QUARTERS):
-                for g in range(GROUPS):
-                    k = GROUPS * p + g
-                    for octet in range(PER_GROUP // 8):
-                        head = base + g * PER_GROUP + octet * 8
-                        u1 = pack[head : head + 8, p : p + 1]
-                        u2 = pack[head : head + 8, DEPTH + p : DEPTH + p + 1]
-                        decay = pack[head : head + 8, 2 * DEPTH : 2 * DEPTH + 1]
-                        for half in range(2):
-                            if row == 1:
-                                chunk = octet * 8 // PART
-                                at = half * PART + octet * 8 - chunk * PART
-                                held = (moved_a, moved_b)[chunk][k, at : at + 8, :]
-                            else:
-                                held = kept_in[
-                                    k,
-                                    octet * 8 : octet * 8 + 8,
-                                    half * LANES : (half + 1) * LANES,
-                                ]
-                            at = half * GROUPS + g
-                            result[
-                                row,
-                                k,
-                                octet * 8 : octet * 8 + 8,
-                                half * LANES : (half + 1) * LANES,
-                            ] = (
-                                held * decay + u1 * b[0][at : at + 1, :] + u2 * b[1][at : at + 1, :]
-                            )
-            write = pltpu.make_async_copy(
-                result.at[row, piece_range(q)],
-                state_out.at[slots[row], piece_range(q)],
-                part_sem.at[3 + row, q],
-            )
-            write.start()
-            writes.append(write)
-        slot = slots[row]
+    for load, (row, q) in zip(loads, parts):
+        load.wait()
+        write = pltpu.make_async_copy(
+            held.at[row, pl.ds(q * size, size)],
+            state_out.at[slots[row], pl.ds(q * size, size)],
+            part_sem.at[2 + row, q],
+        )
+        write.start()
+        writes.append(write)
+    for load in small_loads:
+        load.wait()
+    same_group = (
+        lax.broadcasted_iota(jnp.int32, (LANES, LANES), 0) // PER_GROUP
+        == lax.broadcasted_iota(jnp.int32, (LANES, LANES), 1) // PER_GROUP
+    ).astype(jnp.float32)
+    totals = jnp.dot(
+        sums[0] + sums[1] + sums[2] + sums[3],
+        same_group,
+        preferred_element_type=jnp.float32,
+        precision=lax.Precision.HIGHEST,
+    )
+    factor = lax.rsqrt(totals / (DEPTH * TP * PER_GROUP) + EPSILON)
+    for row, slot in enumerate(slots):
+        live = active[slot] == 1
         for s in range(STEPS):
+            scale = factor[row * STEPS + s : row * STEPS + s + 1, :]
             at = Y_ROWS + (row * STEPS + s) * DEPTH
-            y[s, slot] = pack[at : at + DEPTH, :].astype(jnp.bfloat16)
+            scaled = pack[at : at + DEPTH, :] * scale * norm_gain[...]
+            y[s, slot] = jnp.where(live, scaled, 0.0).astype(jnp.bfloat16)
         for k in range(3):
             at = TAIL_X + (row * 3 + k) * DEPTH
             tail_x[slot, k] = pack[at : at + DEPTH, :].astype(jnp.bfloat16)
@@ -575,7 +563,7 @@
                     [pack[at : at + 4, :], pack[at + 4 : at + 8, :]], axis=1
                 ).astype(jnp.bfloat16)
     for i, (vmem, hbm) in enumerate(((tail_x, tail_x_out), (tail_bc, tail_bc_out), (y, y_out))):
-        write = pltpu.make_async_copy(vmem, hbm, sem.at[2 + i])
+        write = pltpu.make_async_copy(vmem, hbm, sem.at[5 + i])
         write.start()
         writes.append(write)
     for write in writes:
@@ -621,17 +609,16 @@
         dt_bias.reshape(1, -1),
         a_log.reshape(1, -1),
         skip_d.reshape(1, -1),
-        norm_gain,
     )
     long_buffer = pltpu.VMEM((devices, 2 * PART + TAIL_ROWS, LANES), jnp.float32)
     short_buffer = pltpu.VMEM((devices, 2 * PART, LANES), jnp.float32)
     hbm = pl.BlockSpec(memory_space=pltpu.HBM)
-    moved_a, moved_b, pack = pl.pallas_call(
+    final, pack, sums = pl.pallas_call(
         functools.partial(relocate_kernel, devices),
         out_shape=(
-            jax.ShapeDtypeStruct(long_buffer.shape, jnp.float32),
-            jax.ShapeDtypeStruct(short_buffer.shape, jnp.float32),
+            jax.ShapeDtypeStruct(pieces.shape, jnp.float32),
             jax.ShapeDtypeStruct((PACK_ROWS, LANES), jnp.float32),
+            jax.ShapeDtypeStruct((TP, 8, LANES), jnp.float32),
         ),
         in_specs=[hbm] * len(operands),
         out_specs=(hbm, hbm, hbm),
@@ -644,50 +631,52 @@
         + [long_buffer, short_buffer] * 4
         + [
             pltpu.VMEM((PACK_ROWS, LANES), jnp.float32),
+            pltpu.VMEM(pieces.shape, jnp.float32),
             pltpu.VMEM((2, STEPS, 2, GROUPS, 8, LANES), jnp.float32),
+            pltpu.VMEM((2, STEPS, 2, GROUPS, 8, LANES), jnp.float32),
+            pltpu.VMEM((2, LANES, LANES), jnp.float32),
             pltpu.VMEM((2, STEPS, DEPTH, LANES), jnp.float32),
             pltpu.VMEM((2, STEPS, DEPTH, LANES), jnp.float32),
             pltpu.VMEM((2, STEPS, DEPTH, LANES), jnp.float32),
             pltpu.VMEM((STEPS, LANES, LANES), jnp.float32),
             pltpu.VMEM((LANES, LANES), jnp.float32),
             pltpu.VMEM((8, LANES), jnp.float32),
-            pltpu.VMEM((TP - 1, 8, LANES), jnp.float32),
             pltpu.SemaphoreType.DMA((len(operands),)),
             pltpu.SemaphoreType.DMA((2, CHUNKS)),
             pltpu.SemaphoreType.DMA((2, CHUNKS)),
             pltpu.SemaphoreType.DMA((TP - 1,)),
             pltpu.SemaphoreType.DMA((TP - 1,)),
-            pltpu.SemaphoreType.DMA((3,)),
+            pltpu.SemaphoreType.DMA((3 + CHUNKS,)),
         ],
         compiler_params=pltpu.CompilerParams(
             collective_id=0, has_side_effects=True, vmem_limit_bytes=60 * 1024 * 1024
         ),
     )(*operands)
     state, window_x, window_bc, y = pl.pallas_call(
-        functools.partial(state_kernel, devices),
+        functools.partial(place_kernel, devices),
         out_shape=(
             jax.ShapeDtypeStruct(pieces.shape, jnp.float32),
             jax.ShapeDtypeStruct(tail_x.shape, tail_x.dtype),
             jax.ShapeDtypeStruct(tail_bc.shape, tail_bc.dtype),
             jax.ShapeDtypeStruct(x_new.shape, jnp.bfloat16),
         ),
-        in_specs=[hbm] * 5,
+        in_specs=[hbm] * 6,
         out_specs=(hbm,) * 4,
         scratch_shapes=[
             pltpu.SMEM(source.shape, jnp.int32),
-            pltpu.VMEM((devices, PER_GROUP, width), jnp.float32),
-            long_buffer,
-            short_buffer,
+            pltpu.SMEM(active.shape, jnp.int32),
+            pltpu.VMEM(norm_gain.shape, jnp.float32),
+            pltpu.VMEM((TP, 8, LANES), jnp.float32),
+            pltpu.VMEM(pieces.shape, jnp.float32),
             pltpu.VMEM((PACK_ROWS, LANES), jnp.float32),
-            pltpu.VMEM(pieces.shape, jnp.float32),
             pltpu.VMEM(tail_x.shape, tail_x.dtype),
             pltpu.VMEM(tail_bc.shape, tail_bc.dtype),
             pltpu.VMEM(x_new.shape, jnp.bfloat16),
-            pltpu.SemaphoreType.DMA((5,)),
-            pltpu.SemaphoreType.DMA((5, QUARTERS)),
+            pltpu.SemaphoreType.DMA((8,)),
+            pltpu.SemaphoreType.DMA((4, PARTS)),
         ],
         compiler_params=pltpu.CompilerParams(vmem_limit_bytes=60 * 1024 * 1024),
-    )(source, pieces, moved_a, moved_b, pack)
+    )(source, active, norm_gain, sums, final, pack)
     return state.reshape(state_in.shape), window_x, window_bc, y
 
 

time: 119 us -> 116 us (0.975)
  Pallas kernels: 118 us -> 115 us
    pallas_call x1, Pallas kernels: 5.49 us -> 3.55 us  [on_device(): pl.pallas_call(functools.partial(place_kernel, devices), out_shape=(jax.S...]
where the time goes in v4:
time: 116 us
  Pallas kernels  115 us (99%)
    pallas_call x1, Pallas kernels, on_device(): pl.pallas_call(functools.partial(relocate_kernel, devices), out_shape=(ja...  112 us
    pallas_call x1, Pallas kernels, on_device(): pl.pallas_call(functools.partial(place_kernel, devices), out_shape=(jax.S...  3.55 us

profile of v4, /device:TPU:24, one launch (start us, length us, event | category | flops | bytes accessed | tf_op | source)
XLA Modules:
  0.0 115.9 jit_solution(7906998666098927996)
XLA Ops:
  0.6 111.7 %shard_map.192 = (f32[2,64,32,256]{3,2,1,0:T(8,128)}, f32[256,128]{1,0:T(8,128)}, f32[4,8,128]{2,1,0:T(8,128)}) custom-call(s32[128]{0:T(128)} %source_hbm.3, s32[2]{0:T(128)} %active_hbm.3, f32[2,64,32,256]{3,2,1,0:T(8,128)} %bitcast.5, bf16[2,3,16,128]{3,2,1,0:T(8,128)(2,1)} %tail_x_hbm.1, bf16[2,3,2,4,256]{4,3,2,1,0:T(4,128)(2,1)} %tail_bc_hbm.1, ...), custom_call_target="tpu_custom_call" | custom-call | tf_op jit(solution)/shard_map/pallas_call | solution.py:616
  112.3 3.6 %shard_map.193 = (f32[2,64,32,256]{3,2,1,0:T(8,128)}, bf16[2,3,16,128]{3,2,1,0:T(8,128)(2,1)}, bf16[2,3,2,4,256]{4,3,2,1,0:T(4,128)(2,1)}, bf16[2,2,16,128]{3,2,1,0:T(8,128)(2,1)}) custom-call(s32[128]{0:T(128)} %source_hbm.3, s32[2]{0:T(128)} %active_hbm.3, f32[16,128]{1,0:T(8,128)} %norm_gain_hbm.1, f32[4,8,128]{2,1,0:T(8,128)} %get-tuple-element.11.sums_hbm, ...), custom_call_target="tpu_custom_call" | custom-call | tf_op jit(solution)/shard_map/pallas_call | solution.py:655

commit v5 on v4

--- a/solution.py
+++ b/solution.py
@@ -10,7 +10,7 @@
 EPSILON = 1e-05
 MESH = pl.DeviceIdType.MESH
 CHUNKS = 2
-TAIL_ROWS = 2
+TAIL_X_ROWS = 48
 LANES = 128
 DEPTH = 16
 GROUPS = 4
@@ -74,6 +74,8 @@
     a_log,
     skip_d,
     tails,
+    quarter,
+    quarters,
     first_a,
     first_b,
     spread_a,
@@ -98,6 +100,8 @@
     recv_sem,
     sum_send_sem,
     sum_recv_sem,
+    share_send_sem,
+    share_recv_sem,
     out_sem,
 ):
     me = lax.axis_index("rows")
@@ -193,13 +197,15 @@
             device_id_type=MESH,
         )
 
+    share = TAIL_X_ROWS // TP
+
     def fill(chunk, piece, into, at):
         rows = state[given, piece, chunk * PART : (chunk + 1) * PART, :]
         into[at, 0:PART, :] = rows[:, :LANES]
         into[at, PART : 2 * PART, :] = rows[:, LANES:]
         if chunk == 0:
-            into[at, 2 * PART, :] = tails[piece, :]
-            into[at, 2 * PART + 1, :] = tails[64 + lax.rem(piece, 32), :]
+            entry = TAIL_X_ROWS + share * column + lax.rem(piece, share)
+            into[at, 2 * PART, :] = tails[jnp.where(piece < TAIL_X_ROWS, piece, entry), :]
 
     loads[3].wait()
     pl.semaphore_wait(barrier, devices - 1 + TP - 1)
@@ -396,11 +402,30 @@
         if chunk == 0:
 
             def untail(k, carry):
-                tails[64 + lax.rem(k, 32), :] = back_a[k, 2 * PART + 1, :]
                 tails[k, :] = back_a[k, 2 * PART, :]
                 return carry
 
             lax.fori_loop(0, devices, untail, 0)
+            quarter[...] = tails[TAIL_X_ROWS : TAIL_X_ROWS + 16, :]
+            quarters[column] = quarter[...]
+            shares = [
+                pltpu.make_async_remote_copy(
+                    src_ref=quarter,
+                    dst_ref=quarters.at[column],
+                    send_sem=share_send_sem.at[j - 1],
+                    recv_sem=share_recv_sem.at[j - 1],
+                    device_id={"tp": lax.rem(column + j, TP)},
+                    device_id_type=MESH,
+                )
+                for j in range(1, TP)
+            ]
+            for copy in shares:
+                copy.start()
+            for copy in shares:
+                copy.wait()
+            for r in range(TAIL_X_ROWS):
+                at = TAIL_X_ROWS + r
+                tails[at : at + 1, :] = quarters[r // share, r % share : r % share + 1, :]
             window_bc = [
                 [
                     jnp.concatenate(
@@ -610,7 +635,7 @@
         a_log.reshape(1, -1),
         skip_d.reshape(1, -1),
     )
-    long_buffer = pltpu.VMEM((devices, 2 * PART + TAIL_ROWS, LANES), jnp.float32)
+    long_buffer = pltpu.VMEM((devices, 2 * PART + 1, LANES), jnp.float32)
     short_buffer = pltpu.VMEM((devices, 2 * PART, LANES), jnp.float32)
     hbm = pl.BlockSpec(memory_space=pltpu.HBM)
     final, pack, sums = pl.pallas_call(
@@ -627,7 +652,11 @@
             pltpu.SMEM(active.shape, jnp.int32),
         ]
         + [pltpu.VMEM(a.shape, a.dtype) for a in operands[2:]]
-        + [pltpu.VMEM((96, LANES), jnp.float32)]
+        + [
+            pltpu.VMEM((2 * TAIL_X_ROWS, LANES), jnp.float32),
+            pltpu.VMEM((16, LANES), jnp.float32),
+            pltpu.VMEM((TP, 16, LANES), jnp.float32),
+        ]
         + [long_buffer, short_buffer] * 4
         + [
             pltpu.VMEM((PACK_ROWS, LANES), jnp.float32),
@@ -644,6 +673,8 @@
             pltpu.SemaphoreType.DMA((len(operands),)),
             pltpu.SemaphoreType.DMA((2, CHUNKS)),
             pltpu.SemaphoreType.DMA((2, CHUNKS)),
+            pltpu.SemaphoreType.DMA((TP - 1,)),
+            pltpu.SemaphoreType.DMA((TP - 1,)),
             pltpu.SemaphoreType.DMA((TP - 1,)),
             pltpu.SemaphoreType.DMA((TP - 1,)),
             pltpu.SemaphoreType.DMA((3 + CHUNKS,)),

time: 116 us -> 115 us (level)
    pallas_call x1, Pallas kernels: 112 us -> 110 us  [on_device(): pl.pallas_call(functools.partial(relocate_kernel, devices), out_shape=(ja...]
where the time goes in v5:
time: 115 us
  Pallas kernels  114 us (99%)
    pallas_call x1, Pallas kernels, on_device(): pl.pallas_call(functools.partial(relocate_kernel, devices), out_shape=(ja...  110 us
    pallas_call x1, Pallas kernels, on_device(): pl.pallas_call(functools.partial(place_kernel, devices), out_shape=(jax.S...  3.55 us

profile of v5, /device:TPU:24, one launch (start us, length us, event | category | flops | bytes accessed | tf_op | source)
XLA Modules:
  0.0 114.6 jit_solution(685093214958703416)
XLA Ops:
  0.6 110.4 %shard_map.192 = (f32[2,64,32,256]{3,2,1,0:T(8,128)}, f32[256,128]{1,0:T(8,128)}, f32[4,8,128]{2,1,0:T(8,128)}) custom-call(s32[128]{0:T(128)} %source_hbm.3, s32[2]{0:T(128)} %active_hbm.3, f32[2,64,32,256]{3,2,1,0:T(8,128)} %bitcast.5, bf16[2,3,16,128]{3,2,1,0:T(8,128)(2,1)} %tail_x_hbm.1, bf16[2,3,2,4,256]{4,3,2,1,0:T(4,128)(2,1)} %tail_bc_hbm.1, ...), custom_call_target="tpu_custom_call" | custom-call | tf_op jit(solution)/shard_map/pallas_call | solution.py:641
  111.1 3.6 %shard_map.193 = (f32[2,64,32,256]{3,2,1,0:T(8,128)}, bf16[2,3,16,128]{3,2,1,0:T(8,128)(2,1)}, bf16[2,3,2,4,256]{4,3,2,1,0:T(4,128)(2,1)}, bf16[2,2,16,128]{3,2,1,0:T(8,128)(2,1)}) custom-call(s32[128]{0:T(128)} %source_hbm.3, s32[2]{0:T(128)} %active_hbm.3, f32[16,128]{1,0:T(8,128)} %norm_gain_hbm.1, f32[4,8,128]{2,1,0:T(8,128)} %get-tuple-element.11.sums_hbm, ...), custom_call_target="tpu_custom_call" | custom-call | tf_op jit(solution)/shard_map/pallas_call | solution.py:686

commit v6 on v5

--- a/solution.py
+++ b/solution.py
@@ -135,7 +135,7 @@
             )
         )
     ]
-    for load in loads:
+    for load in loads[:4]:
         load.start()
     barrier = pltpu.get_barrier_semaphore()
 
@@ -157,6 +157,8 @@
             device_id_type=MESH,
         )
 
+    for load in loads[4:]:
+        load.start()
     loads[0].wait()
     low = source[2 * me]
     high = source[2 * me + 1]
@@ -207,18 +209,26 @@
             entry = TAIL_X_ROWS + share * column + lax.rem(piece, share)
             into[at, 2 * PART, :] = tails[jnp.where(piece < TAIL_X_ROWS, piece, entry), :]
 
+    def ready(chunk):
+        def one(i, carry):
+            to = partner_of(me, i, devices)
+            fill(chunk, to, first[chunk], to)
+            return carry
+
+        lax.fori_loop(1, devices, one, 0)
+        fill(chunk, me, spread[chunk], me)
+
     loads[3].wait()
+    for chunk in range(CHUNKS):
+        ready(chunk)
     pl.semaphore_wait(barrier, devices - 1 + TP - 1)
     for chunk in range(CHUNKS):
 
         def begin(i, carry, chunk=chunk):
-            to = partner_of(me, i, devices)
-            fill(chunk, to, first[chunk], to)
-            remote(0, chunk, to).start()
+            remote(0, chunk, partner_of(me, i, devices)).start()
             return carry
 
         lax.fori_loop(1, devices, begin, 0)
-        fill(chunk, me, spread[chunk], me)
 
     for load in loads[4:]:
         load.wait()

time: 115 us -> 114 us (level)
  no operation moved by 1% of the time
where the time goes in v6:
time: 114 us
  Pallas kernels  114 us (100%)
    pallas_call x1, Pallas kernels, on_device(): pl.pallas_call(functools.partial(relocate_kernel, devices), out_shape=(ja...  110 us
    pallas_call x1, Pallas kernels, on_device(): pl.pallas_call(functools.partial(place_kernel, devices), out_shape=(jax.S...  3.55 us

profile of v6, /device:TPU:24, one launch (start us, length us, event | category | flops | bytes accessed | tf_op | source)
XLA Modules:
  0.0 114.3 jit_solution(1922099914362024966)
XLA Ops:
  0.6 110.1 %shard_map.192 = (f32[2,64,32,256]{3,2,1,0:T(8,128)}, f32[256,128]{1,0:T(8,128)}, f32[4,8,128]{2,1,0:T(8,128)}) custom-call(s32[128]{0:T(128)} %source_hbm.3, s32[2]{0:T(128)} %active_hbm.3, f32[2,64,32,256]{3,2,1,0:T(8,128)} %bitcast.5, bf16[2,3,16,128]{3,2,1,0:T(8,128)(2,1)} %tail_x_hbm.1, bf16[2,3,2,4,256]{4,3,2,1,0:T(4,128)(2,1)} %tail_bc_hbm.1, ...), custom_call_target="tpu_custom_call" | custom-call | tf_op jit(solution)/shard_map/pallas_call | solution.py:651
  110.7 3.6 %shard_map.193 = (f32[2,64,32,256]{3,2,1,0:T(8,128)}, bf16[2,3,16,128]{3,2,1,0:T(8,128)(2,1)}, bf16[2,3,2,4,256]{4,3,2,1,0:T(4,128)(2,1)}, bf16[2,2,16,128]{3,2,1,0:T(8,128)(2,1)}) custom-call(s32[128]{0:T(128)} %source_hbm.3, s32[2]{0:T(128)} %active_hbm.3, f32[16,128]{1,0:T(8,128)} %norm_gain_hbm.1, f32[4,8,128]{2,1,0:T(8,128)} %get-tuple-element.11.sums_hbm, ...), custom_call_target="tpu_custom_call" | custom-call | tf_op jit(solution)/shard_map/pallas_call | solution.py:696

commit v7 on v6

--- a/solution.py
+++ b/solution.py
@@ -312,17 +312,16 @@
                 [rows_c[row, s, half, g] for half in range(2)] for s in range(STEPS)
             ]
             for octet in octets:
-                held = [jnp.zeros((8, LANES), jnp.float32) for _ in range(STEPS)]
+                held = jnp.zeros((8, LANES), jnp.float32)
                 for p in range(DEPTH):
                     left, right = piece(GROUPS * p + g, octet)
                     for s in range(STEPS):
                         dot = jnp.sum(
                             left * c[s][0] + right * c[s][1], axis=1, keepdims=True
                         )
-                        held[s] = jnp.where(lane == p, dot, held[s])
-                for s in range(STEPS):
-                    at = pl.multiple_of(g * PER_GROUP + octet * 8, 8)
-                    dots[s, pl.ds(at, 8), :] = held[s]
+                        held = jnp.where(lane == DEPTH * s + p, dot, held)
+                at = pl.multiple_of(g * PER_GROUP + octet * 8, 8)
+                dots[pl.ds(at, 8), :] = held
             return carry
 
         lax.fori_loop(0, GROUPS, one_group, 0)
@@ -353,8 +352,9 @@
         lax.fori_loop(0, GROUPS, one_group, 0)
 
     def finish(row):
+        by_step = jnp.transpose(dots[...])
         for s in range(STEPS):
-            dot = jnp.transpose(dots[s])[0:DEPTH, :]
+            dot = by_step[DEPTH * s : DEPTH * (s + 1), :]
             gated = (decays[row, s] * dot + extras[row, s]) * gates[row, s]
             at = Y_ROWS + (row * STEPS + s) * DEPTH
             pack[at : at + DEPTH, :] = gated
@@ -677,7 +677,7 @@
             pltpu.VMEM((2, STEPS, DEPTH, LANES), jnp.float32),
             pltpu.VMEM((2, STEPS, DEPTH, LANES), jnp.float32),
             pltpu.VMEM((2, STEPS, DEPTH, LANES), jnp.float32),
-            pltpu.VMEM((STEPS, LANES, LANES), jnp.float32),
+            pltpu.VMEM((LANES, LANES), jnp.float32),
             pltpu.VMEM((LANES, LANES), jnp.float32),
             pltpu.VMEM((8, LANES), jnp.float32),
             pltpu.SemaphoreType.DMA((len(operands),)),

time: 114 us -> 114 us (level)
  no operation moved by 1% of the time
where the time goes in v7:
time: 114 us
  Pallas kernels  114 us (100%)
    pallas_call x1, Pallas kernels, on_device(): pl.pallas_call(functools.partial(relocate_kernel, devices), out_shape=(ja...  110 us
    pallas_call x1, Pallas kernels, on_device(): pl.pallas_call(functools.partial(place_kernel, devices), out_shape=(jax.S...  3.55 us

profile of v7, /device:TPU:24, one launch (start us, length us, event | category | flops | bytes accessed | tf_op | source)
XLA Modules:
  0.0 114.3 jit_solution(8977409639746291266)
XLA Ops:
  0.6 110.1 %shard_map.192 = (f32[2,64,32,256]{3,2,1,0:T(8,128)}, f32[256,128]{1,0:T(8,128)}, f32[4,8,128]{2,1,0:T(8,128)}) custom-call(s32[128]{0:T(128)} %source_hbm.3, s32[2]{0:T(128)} %active_hbm.3, f32[2,64,32,256]{3,2,1,0:T(8,128)} %bitcast.5, bf16[2,3,16,128]{3,2,1,0:T(8,128)(2,1)} %tail_x_hbm.1, bf16[2,3,2,4,256]{4,3,2,1,0:T(4,128)(2,1)} %tail_bc_hbm.1, ...), custom_call_target="tpu_custom_call" | custom-call | tf_op jit(solution)/shard_map/pallas_call | solution.py:651
  110.7 3.6 %shard_map.193 = (f32[2,64,32,256]{3,2,1,0:T(8,128)}, bf16[2,3,16,128]{3,2,1,0:T(8,128)(2,1)}, bf16[2,3,2,4,256]{4,3,2,1,0:T(4,128)(2,1)}, bf16[2,2,16,128]{3,2,1,0:T(8,128)(2,1)}) custom-call(s32[128]{0:T(128)} %source_hbm.3, s32[2]{0:T(128)} %active_hbm.3, f32[16,128]{1,0:T(8,128)} %norm_gain_hbm.1, f32[4,8,128]{2,1,0:T(8,128)} %get-tuple-element.11.sums_hbm, ...), custom_call_target="tpu_custom_call" | custom-call | tf_op jit(solution)/shard_map/pallas_call | solution.py:696
